TPU v7x, 32 devices: a whole 2x2x4 slice. The times are simulated.
32 devices in a mesh: fsdp: 4 (over z), seq: 8 (over y, x, core).
Axes of the slice: x: 2, y: 2, z: 4, core: 2. Of those that a mesh axis runs over, the one named last changes fastest.
Arguments:
- block_input: bfloat16 [4, 2048, 2048], P('fsdp', 'seq'), may hold values from -6 to 6
- ln_gain: bfloat16 [2048], P(('fsdp', 'seq')), may hold values from 0.5 to 1.5
- norm_layer_bias: bfloat16 [2048], P(('fsdp', 'seq')), may hold values from -1.796875 to 1.796875
- query_key_value_weight: bfloat16 [2048, 6144], P(('fsdp', 'seq')), may hold values from -0.125 to 0.125
- query_key_value_bias: bfloat16 [6144], P(('fsdp', 'seq')), may hold values from -0.29882812 to 0.29882812
- attention_output_weight: bfloat16 [2048, 2048], P(('fsdp', 'seq')), may hold values from -1.5 to 1.5
- attention_output_bias: bfloat16 [2048], P(('fsdp', 'seq')), may hold values from -1.796875 to 1.796875
- first_feed_weight: bfloat16 [2048, 8192], P(('fsdp', 'seq')), may hold values from -0.125 to 0.125
- first_feed_bias: bfloat16 [8192], P(('fsdp', 'seq')), may hold values from -3 to 3
- second_feed_weight: bfloat16 [8192, 2048], P(('fsdp', 'seq')), may hold values from -0.0625 to 0.0625
- second_feed_bias: bfloat16 [2048], P(('fsdp', 'seq')), may hold values from -1.796875 to 1.796875
- cotangent: bfloat16 [4, 2048, 2048], P('fsdp', 'seq'), may hold values from -6 to 6
Outputs:
- block_output: bfloat16 [4, 2048, 2048], P('fsdp', 'seq')
- grad_input: float32 [4, 2048, 2048], P('fsdp', 'seq')
- norm_gain_gradient: float32 [2048], P(('fsdp', 'seq'))
- grad_ln_bias: float32 [2048], P(('fsdp', 'seq'))
- grad_w_qkv: float32 [2048, 6144], P(('fsdp', 'seq'))
- grad_b_qk: float32 [4096], P(('fsdp', 'seq'))
- grad_b_v: float32 [2048], P(('fsdp', 'seq'))
- grad_w_out: float32 [2048, 2048], P(('fsdp', 'seq'))
- grad_b_out: float32 [2048], P(('fsdp', 'seq'))
- grad_w_fc1: float32 [2048, 8192], P(('fsdp', 'seq'))
- grad_b_fc1: float32 [8192], P(('fsdp', 'seq'))
- grad_w_fc2: float32 [8192, 2048], P(('fsdp', 'seq'))
- grad_b_fc2: float32 [2048], P(('fsdp', 'seq'))
All inputs are finite; a program needn't handle non-finite values.
Results may differ from a plain program's by a relative error of at most 0.011.
Values may be sent and summed in bfloat16 or wider, within the bound.
No kernel may reach another device: no remote copies, remote signals or barrier semaphores. Data moves between devices by JAX's collectives and lax.ppermute only.
A program may use at most 448 MiB of HBM per device.

v0:
```python
import jax
import jax.numpy as jnp
from jax import lax
from jax.sharding import PartitionSpec as P

H = 32
HD = 64
ROT = 32


EPSILON = 1e-05


def layer_norm(values, gain, shift):
    average = jnp.mean(values, -1, keepdims=True)
    centred = values - average
    variance = jnp.mean(centred * centred, -1, keepdims=True)
    return centred * lax.rsqrt(variance + EPSILON) * gain + shift


def gelu_tanh(values):
    return (
        0.5
        * values
        * (1.0 + jnp.tanh(0.7978845608028654 * (values + 0.044715 * values * values * values)))
    )


def rotate_heads(projected_rows, positions):
    half_rot = ROT // 2
    freqs = 10000.0 ** (-2.0 * jnp.arange(half_rot).astype(jnp.float32) / ROT)
    angles = positions.astype(jnp.float32)[:, None] * freqs[None, :]
    cosine = jnp.cos(angles)[:, None, :]
    sine = jnp.sin(angles)[:, None, :]
    turned = []
    for which in range(2):
        part = projected_rows[..., which, :, :]
        first = part[..., :half_rot]
        second = part[..., half_rot:ROT]
        turned.append(
            jnp.concatenate(
                [first * cosine - second * sine, second * cosine + first * sine, part[..., ROT:]],
                -1,
            )
        )
    turned.append(projected_rows[..., 2, :, :])
    return jnp.stack(turned, -3)


def block_probs(queries, keys, index, block, scale):
    rows = lax.dynamic_slice_in_dim(queries, index * block, block, 0)
    score_matrix = (
        jnp.einsum("qhd,khd->hqk", rows, keys, preferred_element_type=jnp.float32) * scale
    )
    query_pos = index * block + jnp.arange(block)
    allowed = query_pos[:, None] >= jnp.arange(keys.shape[0])[None, :]
    score_matrix = jnp.where(allowed[None], score_matrix, -1e30)
    row_max = jnp.max(score_matrix, -1, keepdims=True)
    expo = jnp.exp(score_matrix - row_max)
    return (rows, expo / jnp.sum(expo, -1, keepdims=True))


def attend_forward(queries, keys, values, block, scale):
    length = keys.shape[0]

    def one_block(index):
        rows, probs = block_probs(queries, keys, index, block, scale)
        return jnp.einsum(
            "hqk,khd->qhd", probs.astype(jnp.bfloat16), values, preferred_element_type=jnp.float32
        ).astype(jnp.bfloat16)

    outs = lax.map(one_block, jnp.arange(length // block))
    return outs.reshape(length, keys.shape[1] * keys.shape[2])


def attend_backward(queries, keys, values, d_attn, block, scale):
    length = keys.shape[0]

    def one_block(carry, index):
        d_keys, d_values = carry
        rows, probs = block_probs(queries, keys, index, block, scale)
        grad_rows = lax.dynamic_slice_in_dim(d_attn, index * block, block, 0)
        probs_low = probs.astype(jnp.bfloat16)
        d_values = d_values + jnp.einsum(
            "hqk,qhd->khd", probs_low, grad_rows, preferred_element_type=jnp.float32
        )
        d_probs = jnp.einsum("qhd,khd->hqk", grad_rows, values, preferred_element_type=jnp.float32)
        centre = jnp.sum(probs * d_probs, -1, keepdims=True)
        d_scores = (probs * (d_probs - centre)).astype(jnp.bfloat16)
        d_rows = (
            jnp.einsum("hqk,khd->qhd", d_scores, keys, preferred_element_type=jnp.float32) * scale
        )
        d_keys = (
            d_keys
            + jnp.einsum("hqk,qhd->khd", d_scores, rows, preferred_element_type=jnp.float32) * scale
        )
        return ((d_keys, d_values), d_rows)

    zeros = jnp.zeros(keys.shape, jnp.float32)
    (d_keys, d_values), d_rows = lax.scan(one_block, (zeros, zeros), jnp.arange(length // block))
    return (d_rows.reshape(keys.shape), d_keys, d_values)


def local(
    block_input,
    ln_gain,
    norm_layer_bias,
    query_key_value_weight,
    query_key_value_bias,
    attention_output_weight,
    attention_output_bias,
    first_feed_weight,
    first_feed_bias,
    second_feed_weight,
    second_feed_bias,
    cotangent,
):
    gathered = (
        lax.all_gather(ln_gain, ("fsdp", "seq"), axis=0, tiled=True),
        lax.all_gather(norm_layer_bias, ("fsdp", "seq"), axis=0, tiled=True),
        lax.all_gather(query_key_value_weight, ("fsdp", "seq"), axis=0, tiled=True),
        lax.all_gather(query_key_value_bias, ("fsdp", "seq"), axis=0, tiled=True),
        lax.all_gather(attention_output_weight, ("fsdp", "seq"), axis=0, tiled=True),
        lax.all_gather(attention_output_bias, ("fsdp", "seq"), axis=0, tiled=True),
        lax.all_gather(first_feed_weight, ("fsdp", "seq"), axis=0, tiled=True),
        lax.all_gather(first_feed_bias, ("fsdp", "seq"), axis=0, tiled=True),
        lax.all_gather(second_feed_weight, ("fsdp", "seq"), axis=0, tiled=True),
        lax.all_gather(second_feed_bias, ("fsdp", "seq"), axis=0, tiled=True),
    )
    (
        gain_all,
        shift_all,
        wqkv_all,
        bqkv_all,
        wout_all,
        bout_all,
        wfc1_all,
        bfc1_all,
        wfc2_all,
        bfc2_all,
    ) = gathered
    seqs, piece, model_width = block_input.shape
    groups = lax.axis_size("seq")
    length = piece * groups
    local_heads = H // groups
    block = min(512, length)
    scale = HD ** (-0.5)
    tokens = seqs * piece
    inputs = block_input.astype(jnp.float32)
    normed, norm_pull = jax.vjp(
        layer_norm, inputs, gain_all.astype(jnp.float32), shift_all.astype(jnp.float32)
    )
    normalized_reduced = normed.astype(jnp.bfloat16).reshape(tokens, model_width)
    projected_rows = jnp.dot(
        normalized_reduced, wqkv_all, preferred_element_type=jnp.float32
    ) + bqkv_all.astype(jnp.float32)
    positions = lax.axis_index("seq") * piece + jnp.arange(piece)

    def rotate_here(values):
        return rotate_heads(values, positions)

    rotated, rotate_pull = jax.vjp(rotate_here, projected_rows.reshape(seqs, piece, 3, H, HD))
    qkv_low = rotated.astype(jnp.bfloat16).reshape(seqs, piece, 3, model_width)
    by_heads = lax.all_to_all(qkv_low, "seq", split_axis=3, concat_axis=1, tiled=True)
    by_heads = by_heads.reshape(seqs, length, 3, local_heads, HD)

    def forward_one(item):
        return attend_forward(item[:, 0], item[:, 1], item[:, 2], block, scale)

    attn_heads = lax.map(forward_one, by_heads)
    attn_tokens = lax.all_to_all(
        attn_heads, "seq", split_axis=1, concat_axis=2, tiled=True
    ).reshape(tokens, model_width)
    up_preactivation = jnp.dot(
        normalized_reduced, wfc1_all, preferred_element_type=jnp.float32
    ) + bfc1_all.astype(jnp.float32)
    up_activation, gelu_pull = jax.vjp(gelu_tanh, up_preactivation)
    up_low = up_activation.astype(jnp.bfloat16)
    mixed = (
        inputs.reshape(tokens, model_width)
        + jnp.dot(attn_tokens, wout_all, preferred_element_type=jnp.float32)
        + bout_all.astype(jnp.float32)
    )
    mixed = (
        mixed
        + jnp.dot(up_low, wfc2_all, preferred_element_type=jnp.float32)
        + bfc2_all.astype(jnp.float32)
    )
    block_output = mixed.astype(jnp.bfloat16).reshape(seqs, piece, model_width)
    wqkv_back, wout_back, wfc1_back, wfc2_back = (
        lax.all_gather(query_key_value_weight, ("fsdp", "seq"), axis=0, tiled=True),
        lax.all_gather(attention_output_weight, ("fsdp", "seq"), axis=0, tiled=True),
        lax.all_gather(first_feed_weight, ("fsdp", "seq"), axis=0, tiled=True),
        lax.all_gather(second_feed_weight, ("fsdp", "seq"), axis=0, tiled=True),
    )
    grad_low = cotangent.reshape(tokens, model_width)
    d_attn = jnp.einsum(
        "td,ed->te", grad_low, wout_back, preferred_element_type=jnp.float32
    ).astype(jnp.bfloat16)
    d_heads = lax.all_to_all(
        d_attn.reshape(seqs, piece, model_width), "seq", split_axis=2, concat_axis=1, tiled=True
    )
    d_heads = d_heads.reshape(seqs, length, local_heads, HD)
    d_up = jnp.einsum("td,fd->tf", grad_low, wfc2_back, preferred_element_type=jnp.float32)
    (d_pre,) = gelu_pull(d_up)
    d_pre_low = d_pre.astype(jnp.bfloat16)

    def backward_one(paired):
        item, grad_item = paired
        d_queries, d_keys, d_values = attend_backward(
            item[:, 0], item[:, 1], item[:, 2], grad_item, block, scale
        )
        return jnp.stack([d_queries, d_keys, d_values], 1).astype(jnp.bfloat16)

    d_qkv_heads = lax.map(backward_one, (by_heads, d_heads)).reshape(
        seqs, length, 3, local_heads * HD
    )
    d_qkv_tokens = lax.all_to_all(d_qkv_heads, "seq", split_axis=1, concat_axis=3, tiled=True)
    (d_unrotated,) = rotate_pull(d_qkv_tokens.reshape(seqs, piece, 3, H, HD).astype(jnp.float32))
    d_proj = d_unrotated.astype(jnp.bfloat16).reshape(tokens, 3 * model_width)
    d_normed = jnp.einsum("te,de->td", d_proj, wqkv_back, preferred_element_type=jnp.float32)
    d_normed = d_normed + jnp.einsum(
        "tf,df->td", d_pre_low, wfc1_back, preferred_element_type=jnp.float32
    )
    d_inputs, grad_gain, grad_shift = norm_pull(d_normed.reshape(seqs, piece, model_width))
    grad_input = cotangent.astype(jnp.float32) + d_inputs
    term_wqkv = jnp.einsum(
        "td,te->de", normalized_reduced, d_proj, preferred_element_type=jnp.float32
    )
    query_key_value_bias_term = jnp.sum(d_proj.astype(jnp.float32), 0)
    query_key_bias_term = query_key_value_bias_term[: 2 * model_width]
    term_bv = query_key_value_bias_term[2 * model_width :]
    term_wout = jnp.einsum("td,te->de", attn_tokens, grad_low, preferred_element_type=jnp.float32)
    term_bout = jnp.sum(grad_low.astype(jnp.float32), 0)
    attn_summed = (
        lax.psum_scatter(grad_gain, ("fsdp", "seq"), scatter_dimension=0, tiled=True),
        lax.psum_scatter(grad_shift, ("fsdp", "seq"), scatter_dimension=0, tiled=True),
        lax.psum_scatter(term_wqkv, ("fsdp", "seq"), scatter_dimension=0, tiled=True),
        lax.psum_scatter(query_key_bias_term, ("fsdp", "seq"), scatter_dimension=0, tiled=True),
        lax.psum_scatter(term_bv, ("fsdp", "seq"), scatter_dimension=0, tiled=True),
        lax.psum_scatter(term_wout, ("fsdp", "seq"), scatter_dimension=0, tiled=True),
        lax.psum_scatter(term_bout, ("fsdp", "seq"), scatter_dimension=0, tiled=True),
    )
    term_wfc1 = jnp.einsum(
        "td,tf->df", normalized_reduced, d_pre_low, preferred_element_type=jnp.float32
    )
    term_bfc1 = jnp.sum(d_pre_low.astype(jnp.float32), 0)
    term_wfc2 = jnp.einsum("tf,td->fd", up_low, grad_low, preferred_element_type=jnp.float32)
    mlp_summed = (
        lax.psum_scatter(term_wfc1, ("fsdp", "seq"), scatter_dimension=0, tiled=True),
        lax.psum_scatter(term_bfc1, ("fsdp", "seq"), scatter_dimension=0, tiled=True),
        lax.psum_scatter(term_wfc2, ("fsdp", "seq"), scatter_dimension=0, tiled=True),
    )
    return (
        block_output,
        grad_input,
        attn_summed[0],
        attn_summed[1],
        attn_summed[2],
        attn_summed[3],
        attn_summed[4],
        attn_summed[5],
        attn_summed[6],
        mlp_summed[0],
        mlp_summed[1],
        mlp_summed[2],
        attn_summed[6],
    )


def solution(mesh):
    return jax.shard_map(
        local,
        mesh=mesh,
        in_specs=(
            P("fsdp", "seq", None),
            P(("fsdp", "seq")),
            P(("fsdp", "seq")),
            P(("fsdp", "seq"), None),
            P(("fsdp", "seq")),
            P(("fsdp", "seq"), None),
            P(("fsdp", "seq")),
            P(("fsdp", "seq"), None),
            P(("fsdp", "seq")),
            P(("fsdp", "seq"), None),
            P(("fsdp", "seq")),
            P("fsdp", "seq", None),
        ),
        out_specs=(
            P("fsdp", "seq", None),
            P("fsdp", "seq", None),
            P(("fsdp", "seq")),
            P(("fsdp", "seq")),
            P(("fsdp", "seq"), None),
            P(("fsdp", "seq")),
            P(("fsdp", "seq")),
            P(("fsdp", "seq"), None),
            P(("fsdp", "seq")),
            P(("fsdp", "seq"), None),
            P(("fsdp", "seq")),
            P(("fsdp", "seq"), None),
            P(("fsdp", "seq")),
        ),
        check_vma=False,
    )
```

profile of v0, /device:TPU:0, one launch (start us, length us, event | category | flops | bytes accessed | tf_op | source)
XLA Modules:
  0.0 3129.7 jit_solution(4513929575158068800)
XLA Ops:
  11.4 43.7 %all-reduce.21 = (bf16[6144]{0:T(1024)(128)(2,1)S(1)}, bf16[2048]{0:T(1024)(128)(2,1)S(1)}, bf16[2048]{0:T(1024)(128)(2,1)S(1)}, bf16[2048]{0:T(1024)(128)(2,1)}, bf16[2048]{0:T(1024)(128)(2,1)}) all-reduce(bf16[6144]{0:T(1024)(128)(2,1)S(1)} %dynamic-update-slice.2, ...), channel_id=1, replica_groups=mesh['fsdp'=4,'seq'=8] {'fsdp','seq'}, use_global_device_ids=true, to_apply=%add.11 | all-reduce | flops 14336 | bytes 57344
  56.4 35.0 %all-gather.8.cloned.1.call-done = bf16[2048,2048]{1,0:T(8,128)(2,1)} async-done(((bf16[64,2048]{1,0:T(8,128)(2,1)}), bf16[2048,2048]{1,0:T(8,128)(2,1)}) %all-gather.8.cloned.1.call-update) | async-done | bytes 8388624 | tf_op jit(solution)/shard_map/all_gather | solution.py:123
  121.0 132.4 %all-gather.6.cloned.1.call-done = bf16[2048,6144]{1,0:T(8,128)(2,1)} async-done(((bf16[64,6144]{1,0:T(8,128)(2,1)}), bf16[2048,6144]{1,0:T(8,128)(2,1)}) %all-gather.6.cloned.1.call-update) | async-done | bytes 25165840 | tf_op jit(solution)/shard_map/all_gather | solution.py:121
  278.9 17.2 copy.64
  308.0 65.0 %all-to-all-done = bf16[1,256,3,2048]{1,2,0,3:T(4,128)(2,1)} async-done(((bf16[1,256,3,2048]{1,2,0,3:T(4,128)(2,1)}), bf16[1,256,3,2048]{1,2,0,3:T(4,128)(2,1)}, u32[]{:S(2)}, u32[]{:S(2)}) %all-to-all-start) | async-done | bytes 3145760 | tf_op jit(solution)/shard_map/all_to_all | solution.py:164
  389.5 92.4 %while.41 = (s32[]{:T(128)}, bf16[4,512,4,64]{1,3,2,0:T(8,128)(2,1)}, s32[4]{0:T(128)S(1)}, bf16[2048,4,64]{0,2,1:T(8,128)(2,1)}, bf16[2048,4,64]{0,2,1:T(8,128)...) while((s32[]{:T(128)}, ...), condition=%wide.region_5.6_spmd, body=%wide.region_2.5_spmd.sunk | while | flops 1100089856 | bytes 38294184 | solution.py:72
  513.6 243.0 %while.42 = (s32[]{:T(128)}, f32[2048,4,64]{0,2,1:T(8,128)S(1)}, f32[2048,4,64]{0,2,1:T(8,128)}, bf16[4,512,4,64]{1,3,2,0:T(8,128)(2,1)}, s32[4]{0:T(128)S(1)}, ...) while((s32[]{:T(128)}, f32[2048,4,64]{0,2,1:T(8,128)S(1)}, ...), condition=%wide.region_10.11_spmd.clone, body=%wide.region_6.0_spmd.clone.sunk | while | flops 2742682112 | bytes 233361808 | solution.py:100
  527.2 13.6 multiply_reduce_fusion.2
  575.7 14.3 fusion.170
  590.0 13.6 multiply_reduce_fusion.2
  649.9 13.6 multiply_reduce_fusion.2
  772.4 82.0 %all-gather = bf16[32,1,256]{2,1,0:T(2,128)(2,1)S(1)} all-gather(bf16[1,1,256]{2,1,0:T(2,128)(2,1)S(1)} %reshape.414), channel_id=1, replica_groups=mesh['fsdp'=4,'seq'=8] {'fsdp','seq'}, dimensions={0}, use_global_device_ids=true | all-gather | bytes 16896 | tf_op jit(solution)/shard_map/all_gather | solution.py:126
  885.3 13.6 fusion.114
  898.9 17.2 convolution_add_fusion
  916.2 23.0 convert_reduce_fusion
  939.1 16.7 fusion.84
  968.0 22.1 fusion.99
  990.2 25.6 fusion.97
  1015.9 27.7 fusion.86
  1053.8 19.9 fusion.77
  1084.8 179.9 %reduce-scatter.7.cloned.1.call-done = f32[64,2048]{1,0:T(8,128)} async-done(((f32[2048,2048]{1,0:T(8,128)}), f32[64,2048]{1,0:T(8,128)}) %reduce-scatter.7.cloned.1.call-update) | async-done | bytes 524304 | tf_op jit(solution)/shard_map/reduce_scatter | solution.py:241
  1264.7 440.0 %reduce-scatter.5.cloned.1.call-done = f32[64,6144]{1,0:T(8,128)} async-done(((f32[2048,6144]{1,0:T(8,128)}), f32[64,6144]{1,0:T(8,128)}) %reduce-scatter.5.cloned.1.call-update) | async-done | bytes 1572880 | tf_op jit(solution)/shard_map/reduce_scatter | solution.py:238
  1704.7 704.5 %reduce-scatter.9.cloned.1.call-done = f32[64,8192]{1,0:T(8,128)} async-done(((f32[2048,8192]{1,0:T(8,128)}), f32[64,8192]{1,0:T(8,128)}) %reduce-scatter.9.cloned.1.call-update) | async-done | bytes 2097168 | tf_op jit(solution)/shard_map/reduce_scatter | solution.py:250
  2409.3 713.2 %reduce-scatter.11.cloned.1.call-done = f32[256,2048]{1,0:T(8,128)} async-done(((f32[8192,2048]{1,0:T(8,128)}), f32[256,2048]{1,0:T(8,128)}) %reduce-scatter.11.cloned.1.call-update) | async-done | bytes 2097168 | tf_op jit(solution)/shard_map/reduce_scatter | solution.py:252
  (292 shorter events, 475.7 us)
Async XLA Ops:
  7.2 47.8 %copy-start.1 = (bf16[1,256,2048]{2,1,0:T(8,128)(2,1)S(1)}, bf16[1,256,2048]{2,1,0:T(8,128)(2,1)}, u32[]{:S(2)}) copy-start(bf16[1,256,2048]{2,1,0:T(8,128)(2,1)} %param.16) | copy-start | bytes 3145732
  7.2 84.2 %copy-start.3 = (bf16[1,256,2048]{2,1,0:T(8,128)(2,1)S(1)}, bf16[1,256,2048]{2,1,0:T(8,128)(2,1)}, u32[]{:S(2)}) copy-start(bf16[1,256,2048]{2,1,0:T(8,128)(2,1)} %param.27) | copy-start | bytes 3145732
  7.3 84.2 %all-gather.8.cloned.1.call-start = ((), (), s32[]{:S(2)}) async-start(), calls=%async_computation.9 | async-start | bytes 8650752 | tf_op jit(solution)/shard_map/all_gather | solution.py:123
  8.0 245.5 %all-gather.6.cloned.1.call-start = ((), (), s32[]{:S(2)}) async-start(), calls=%async_computation.8 | async-start | bytes 25952256 | tf_op jit(solution)/shard_map/all_gather | solution.py:121
  8.7 890.1 %all-gather.10.cloned.1.call-start = ((), (), s32[]{:S(2)}) async-start(), calls=%async_computation.10 | async-start | bytes 34603008 | tf_op jit(solution)/shard_map/all_gather | solution.py:125
  9.5 906.7 %all-gather.12.cloned.1.call-start = ((), (), s32[]{:S(2)}) async-start(), calls=%async_computation.11 | async-start | bytes 34603008 | tf_op jit(solution)/shard_map/all_gather | solution.py:127
  55.0 198.4 %copy-start.7 = (f32[2048]{0:T(1024)}, f32[2048]{0:T(1024)S(1)}, u32[]{:S(2)}) copy-start(f32[2048]{0:T(1024)S(1)} %convert_element_type.121) | copy-start | bytes 24580
  55.0 198.4 %copy-start.11 = (f32[2048]{0:T(1024)}, f32[2048]{0:T(1024)S(1)}, u32[]{:S(2)}) copy-start(f32[2048]{0:T(1024)S(1)} %convert_element_type.122) | copy-start | bytes 24580
  55.3 198.2 %copy-start.13 = (f32[256]{0:T(256)}, f32[256]{0:T(256)S(1)}, u32[]{:S(2)}) copy-start(f32[256]{0:T(256)S(1)} %broadcast_multiply_fusion) | copy-start | bytes 3076
  55.7 197.7 %copy-start.15 = (f32[256]{0:T(256)}, f32[256]{0:T(256)S(1)}, u32[]{:S(2)}) copy-start(f32[256]{0:T(256)S(1)} %fusion.95) | copy-start | bytes 3076
  56.4 221.6 %copy-start.17 = (f32[256,16]{0,1:T(8,128)}, f32[256,16]{0,1:T(8,128)S(1)}, u32[]{:S(2)}) copy-start(f32[256,16]{0,1:T(8,128)S(1)} %get-tuple-element.220) | copy-start | bytes 49156
  56.4 221.6 %copy-start.19 = (f32[256,16]{0,1:T(8,128)}, f32[256,16]{0,1:T(8,128)S(1)}, u32[]{:S(2)}) copy-start(f32[256,16]{0,1:T(8,128)S(1)} %get-tuple-element.221) | copy-start | bytes 49156
  117.0 179.2 %all-to-all-start.2 = ((bf16[8,2,32768]{2,1,0:T(2,128)(2,1)}), bf16[8,2,32768]{2,1,0:T(2,128)(2,1)S(1)}, u32[]{:S(2)}, u32[]{:S(2)}) async-start(bf16[8,2,32768]{2,1,0:T(2,128)(2,1)} %reshape.420), calls=%async_computation.2 | async-start | bytes 2097152 | tf_op jit(solution)/shard_map/all_to_all | solution.py:200
  296.2 76.9 %all-to-all-start = ((bf16[1,256,3,2048]{1,2,0,3:T(4,128)(2,1)}), bf16[1,256,3,2048]{1,2,0,3:T(4,128)(2,1)}, u32[]{:S(2)}, u32[]{:S(2)}) async-start(bf16[1,256,3,2048]{1,2,0,3:T(4,128)(2,1)} %copy.64), calls=%async_computation | async-start | bytes 8388608 | tf_op jit(solution)/shard_map/all_to_all | solution.py:164
  509.0 258.7 %all-to-all-start.1 = ((bf16[8,2,32768]{2,1,0:T(2,128)(2,1)}), bf16[8,2,32768]{2,1,0:T(2,128)(2,1)}, u32[]{:S(2)}, u32[]{:S(2)}) async-start(bf16[8,2,32768]{2,1,0:T(2,128)(2,1)} %reshape.418), calls=%async_computation.1 | async-start | bytes 2097152 | tf_op jit(solution)/shard_map/all_to_all | solution.py:171
  649.9 17.5 slice-start.3
  767.7 86.8 %copy-start.4 = (bf16[1,256,2048]{2,1,0:T(8,128)(2,1)S(1)}, bf16[1,256,2048]{2,1,0:T(8,128)(2,1)}, u32[]{:S(2)}) copy-start(bf16[1,256,2048]{2,1,0:T(8,128)(2,1)} %param.27) | copy-start | bytes 3145732
  767.7 96.4 %all-to-all-start.3 = ((bf16[1,2048,3,256]{3,2,0,1:T(4,128)(2,1)}), bf16[1,2048,3,256]{3,2,0,1:T(4,128)(2,1)}, u32[]{:S(2)}, u32[]{:S(2)}) async-start(bf16[1,2048,3,256]{3,2,0,1:T(4,128)(2,1)} %copy.73), calls=%async_computation.3 | async-start | bytes 8388608 | tf_op jit(solution)/shard_map/all_to_all | solution.py:218
  772.4 305.4 %all-reduce.24.cloned.1.call-start = ((), (), s32[]{:S(2)}) async-start(), calls=%async_computation.16 | async-start | bytes 163840
  958.2 306.5 %reduce-scatter.7.cloned.1.call-start = ((), (), s32[]{:S(2)}) async-start(), calls=%async_computation.13 | async-start | bytes 17301504 | tf_op jit(solution)/shard_map/reduce_scatter | solution.py:241
  968.0 736.7 %reduce-scatter.5.cloned.1.call-start = ((), (), s32[]{:S(2)}) async-start(), calls=%async_computation.12 | async-start | bytes 51904512 | tf_op jit(solution)/shard_map/reduce_scatter | solution.py:238
  990.2 1419.1 %reduce-scatter.9.cloned.1.call-start = ((), (), s32[]{:S(2)}) async-start(), calls=%async_computation.14 | async-start | bytes 69206016 | tf_op jit(solution)/shard_map/reduce_scatter | solution.py:250
  1015.8 2106.7 %reduce-scatter.11.cloned.1.call-start = ((), (), s32[]{:S(2)}) async-start(), calls=%async_computation.15 | async-start | bytes 69206016 | tf_op jit(solution)/shard_map/reduce_scatter | solution.py:252
  1078.5 2044.5 %copy-start.31 = (f32[64]{0:T(128)}, f32[64]{0:T(128)S(1)}, u32[]{:S(2)}) copy-start(f32[64]{0:T(128)S(1)} %dynamic-slice.4) | copy-start | bytes 772
  (46 other events, 398.6 us)
Sparse Core Ops, SparseCore 0:
  10.9 80.4 all-gather.7
  94.3 159.1 all-gather.5
  256.3 217.4 all-gather.9
  476.5 204.3 all-gather.11
  958.3 119.3 all-reduce.23
  1080.4 184.2 reduce-scatter.6
  1271.7 432.9 reduce-scatter.4
  1707.7 701.5 reduce-scatter.8
  2412.2 710.2 reduce-scatter.10
where the time goes:
time: 3140 us; the launch traced here: 3130 us
  waiting for transfers between devices  2280 us (73%)
  matrix products  455 us (14%)
  local copies, waits for them, and re-layouts  141 us (4%)
  blocking collectives  126 us (4%)
  other arithmetic  92.4 us (3%)
    reduce_scatter x1, waiting for transfers between devices, local(): lax.psum_scatter(term_wfc2, ('fsdp', 'seq'), scatter_dimension=0, tiled=T...  713 us
    reduce_scatter x1, waiting for transfers between devices, local(): lax.psum_scatter(term_wfc1, ('fsdp', 'seq'), scatter_dimension=0, tiled=T...  705 us
    reduce_scatter x1, waiting for transfers between devices, local(): lax.psum_scatter(term_wqkv, ('fsdp', 'seq'), scatter_dimension=0, tiled=T...  440 us
    reduce_scatter x1, waiting for transfers between devices, local(): lax.psum_scatter(term_wout, ('fsdp', 'seq'), scatter_dimension=0, tiled=T...  180 us
    all_gather x1, waiting for transfers between devices, local(): lax.all_gather(query_key_value_weight, ('fsdp', 'seq'), axis=0, tiled=True)  132 us
    sub x8, matrix products, block_probs(): expo = jnp.exp(score_matrix - row_max)  89 us
    all_gather x1, blocking collectives, local(): lax.all_gather(first_feed_bias, ('fsdp', 'seq'), axis=0, tiled=True)  82 us
    all_to_all x1, waiting for transfers between devices, local(): lax.all_to_all(qkv_low, 'seq', split_axis=3, concat_axis=1, tiled=True)  65 us
  transfers between devices with their start and end apart: 13, of which 8 were waited for; matrix products, arithmetic and copies ran while one was open for 20% of the time, Pallas kernels for 0%

commit v1 on v0

v1 whole, which is shorter than its diff:
```python
import functools

import jax
import jax.numpy as jnp
from jax import lax
from jax.experimental import pallas as pl
from jax.experimental.pallas import tpu as pltpu
from jax.sharding import PartitionSpec as P

H = 32
HD = 64
ROT = 32
EPSILON = 1e-05
BOTH = ("fsdp", "seq")
f32 = jnp.float32
bf16 = jnp.bfloat16


def dot(a, b, ca, cb):
    return lax.dot_general(a, b, (((ca,), (cb,)), ((), ())), preferred_element_type=f32)


def causal(tile):
    keys = lax.broadcasted_iota(jnp.int32, tile.shape, 0)
    queries = lax.broadcasted_iota(jnp.int32, tile.shape, 1)
    return jnp.where(queries >= keys, tile, -1e30)


def forward_kernel(block, q_ref, k_ref, v_ref, o_ref, lse_ref, kn_ref):
    blocks = q_ref.shape[1] // block
    kn_ref[...] = k_ref[...].T
    for i in range(blocks):
        rows = pl.ds(i * block, block)
        q = q_ref[:, rows] * jnp.asarray(HD**-0.5, bf16)
        best = total = acc = None
        for j in range(i, -1, -1):
            cols = pl.ds(j * block, block)
            s = dot(kn_ref[cols, :], q, 1, 0)
            if j == i:
                s = causal(s)
            top = jnp.max(s, 0, keepdims=True)
            if best is None:
                best = top
                p = jnp.exp(s - best)
                total = jnp.sum(p, 0, keepdims=True)
                acc = dot(v_ref[:, cols], p.astype(bf16), 1, 0)
            else:
                new = jnp.maximum(best, top)
                fade = jnp.exp(best - new)
                p = jnp.exp(s - new)
                total = total * fade + jnp.sum(p, 0, keepdims=True)
                acc = acc * fade + dot(v_ref[:, cols], p.astype(bf16), 1, 0)
                best = new
        o_ref[:, rows] = (acc / total).astype(bf16)
        lse_ref[0, :, rows] = best + jnp.log(total)


def attend_forward(qkv, heads):
    length = qkv.shape[1]
    block = length // 2

    def spec(part):
        return pl.BlockSpec((HD, length), lambda h: (part * heads + h, 0))

    return pl.pallas_call(
        functools.partial(forward_kernel, block),
        grid=(heads,),
        in_specs=[spec(0), spec(1), spec(2)],
        out_specs=[
            pl.BlockSpec((HD, length), lambda h: (h, 0)),
            pl.BlockSpec((1, 1, length), lambda h: (h, 0, 0)),
        ],
        out_shape=[
            jax.ShapeDtypeStruct((heads * HD, length), bf16),
            jax.ShapeDtypeStruct((heads, 1, length), f32),
        ],
        scratch_shapes=[pltpu.VMEM((length, HD), bf16)],
        compiler_params=pltpu.CompilerParams(vmem_limit_bytes=48 << 20),
        cost_estimate=pl.CostEstimate(
            flops=heads * length * length * 1024, bytes_accessed=length * heads * HD * 8, transcendentals=0
        ),
        name="attend_forward",
    )(qkv, qkv, qkv)


def backward_kernel(block, q_ref, k_ref, v_ref, o_ref, g_ref, lse_ref, d_ref, kn_ref, vn_ref, dk_acc, dv_acc):
    blocks = q_ref.shape[1] // block
    kn_ref[...] = k_ref[...].T
    vn_ref[...] = v_ref[...].T
    for i in range(blocks):
        rows = pl.ds(i * block, block)
        q = q_ref[:, rows] * jnp.asarray(HD**-0.5, bf16)
        g = g_ref[:, rows]
        lse = lse_ref[0, :, rows]
        delta = jnp.sum(g.astype(f32) * o_ref[:, rows].astype(f32), 0, keepdims=True)
        dq = None
        for j in range(i, -1, -1):
            cols = pl.ds(j * block, block)
            s = dot(kn_ref[cols, :], q, 1, 0)
            if j == i:
                s = causal(s)
            p = jnp.exp(s - lse)
            dp = dot(vn_ref[cols, :], g, 1, 0)
            ds = (p * (dp - delta)).astype(bf16)
            dv = dot(g, p.astype(bf16), 1, 1)
            dk = dot(q, ds, 1, 1)
            if j == i:
                dv_acc[:, cols] = dv
                dk_acc[:, cols] = dk
            else:
                dv_acc[:, cols] += dv
                dk_acc[:, cols] += dk
            part = dot(k_ref[:, cols], ds, 1, 0)
            dq = part if dq is None else dq + part
        d_ref[0, 0, :, rows] = (dq * (HD**-0.5)).astype(bf16)
    d_ref[1, 0] = dk_acc[...].astype(bf16)
    d_ref[2, 0] = dv_acc[...].astype(bf16)


def attend_backward(qkv, attn, d_attn, lse, heads):
    length = qkv.shape[1]
    block = length // 4

    def spec(part):
        return pl.BlockSpec((HD, length), lambda h: (part * heads + h, 0))

    return pl.pallas_call(
        functools.partial(backward_kernel, block),
        grid=(heads,),
        in_specs=[
            spec(0),
            spec(1),
            spec(2),
            spec(0),
            spec(0),
            pl.BlockSpec((1, 1, length), lambda h: (h, 0, 0)),
        ],
        out_specs=pl.BlockSpec((3, 1, HD, length), lambda h: (0, h, 0, 0)),
        out_shape=jax.ShapeDtypeStruct((3, heads, HD, length), bf16),
        scratch_shapes=[pltpu.VMEM((length, HD), bf16)] * 2 + [pltpu.VMEM((HD, length), f32)] * 2,
        compiler_params=pltpu.CompilerParams(vmem_limit_bytes=48 << 20),
        cost_estimate=pl.CostEstimate(
            flops=heads * length * length * 2048, bytes_accessed=length * heads * HD * 16, transcendentals=0
        ),
        name="attend_backward",
    )(qkv, qkv, qkv, attn, d_attn, lse)


def normalise(values):
    average = jnp.mean(values, -1, keepdims=True)
    centred = values - average
    variance = jnp.mean(centred * centred, -1, keepdims=True)
    inverse = lax.rsqrt(variance + EPSILON)
    return centred * inverse, inverse


def gelu_tanh(values):
    return 0.5 * values * (1.0 + jnp.tanh(0.7978845608028654 * (values + 0.044715 * values * values * values)))


def rotate(parts, cosine, sine):
    half = ROT // 2
    first, second = parts[..., :half, :], parts[..., half:ROT, :]
    return jnp.concatenate(
        [first * cosine - second * sine, second * cosine + first * sine, parts[..., ROT:, :]], -2
    )


def swap(value, axes, size, bit):
    return lax.ppermute(value, axes, [(i, i ^ bit) for i in range(size)])


def gather_small(values, size):
    index = lax.axis_index(BOTH)
    block = values[None]
    bit = 1
    while bit < size:
        other = swap(block, BOTH, size, bit)
        high = (index & bit) > 0
        block = jnp.concatenate([jnp.where(high, other, block), jnp.where(high, block, other)], 0)
        bit *= 2
    return block


def scatter_small(values, size):
    index = lax.axis_index(BOTH)
    block = values
    bit = size // 2
    while bit:
        high = (index & bit) > 0
        low_half, high_half = block[:bit], block[bit:]
        other = swap(jnp.where(high, low_half, high_half), BOTH, size, bit)
        block = jnp.where(high, high_half, low_half) + other
        bit //= 2
    return block[0]


def gather_tokens(own, groups):
    if groups != 8:
        return lax.all_gather(own, "seq", axis=0, tiled=True)
    index = lax.axis_index("seq")
    core, place = index % 2, index // 2
    by_x = swap(own, "seq", 8, 2)
    by_y = swap(own, "seq", 8, 4)
    relay = jnp.where(core == 0, by_y, by_x)
    diagonal = lax.ppermute(relay, "seq", [(i, i ^ (4 if i % 2 else 2)) for i in range(8)])
    mine = jnp.zeros((4, *own.shape), own.dtype)
    for shift, piece in ((0, own), (1, by_x), (2, by_y), (3, diagonal)):
        mine = lax.dynamic_update_index_in_dim(mine, piece, place ^ shift, 0)
    other = swap(mine, "seq", 8, 1)
    both = jnp.zeros((4, 2, *own.shape), own.dtype)
    both = lax.dynamic_update_index_in_dim(both, mine, core, 1)
    both = lax.dynamic_update_index_in_dim(both, other, 1 - core, 1)
    return both.reshape(groups * own.shape[0], *own.shape[1:])


def take(values, index, axis):
    return lax.dynamic_index_in_dim(values, index, axis, keepdims=False)


def scatter_tokens(terms, groups):
    if groups != 8:
        return lax.psum_scatter(terms, "seq", scatter_dimension=0, tiled=True).astype(f32)
    rows, width = terms.shape[0] // groups, terms.shape[1]
    index = lax.axis_index("seq")
    core, x, y = index % 2, (index // 2) % 2, index // 4
    cells = terms.reshape(2, 2, 2, rows, width)
    got = swap(take(cells, 1 - core, 2), "seq", 8, 1)
    cells = take(cells, core, 2).astype(f32) + got.astype(f32)
    half = width // 2
    left, right = cells[..., :half], cells[..., half:]
    got_left = swap(take(left, 1 - x, 1).astype(bf16), "seq", 8, 2)
    got_right = swap(take(right, 1 - y, 0).astype(bf16), "seq", 8, 4)
    left = take(left, x, 1) + got_left.astype(f32)
    right = take(right, y, 0) + got_right.astype(f32)
    got_left = swap(take(left, 1 - y, 0).astype(bf16), "seq", 8, 4)
    got_right = swap(take(right, 1 - x, 0).astype(bf16), "seq", 8, 2)
    left = take(left, y, 0) + got_left.astype(f32)
    right = take(right, x, 0) + got_right.astype(f32)
    return jnp.concatenate([left, right], -1)


def to_columns(weight, groups):
    rows, blocks, _, width = weight.shape
    sent = weight.transpose(2, 0, 1, 3).reshape(groups * rows, blocks * width)
    return lax.all_to_all(sent, "seq", split_axis=0, concat_axis=0, tiled=True)


def to_rows(grads, groups, blocks):
    rows, width = grads.shape[0] // groups, grads.shape[1] // blocks
    got = lax.all_to_all(grads, "seq", split_axis=0, concat_axis=0, tiled=True)
    return got.reshape(groups, rows, blocks, width).transpose(1, 2, 0, 3)


def local(
    block_input,
    ln_gain,
    norm_layer_bias,
    query_key_value_weight,
    query_key_value_bias,
    attention_output_weight,
    attention_output_bias,
    first_feed_weight,
    first_feed_bias,
    second_feed_weight,
    second_feed_bias,
    cotangent,
):
    shards, groups = lax.axis_size("fsdp"), lax.axis_size("seq")
    size = shards * groups
    me = lax.axis_index("seq")
    _, piece, width = block_input.shape
    length = piece * groups
    heads = H // groups
    rows = query_key_value_weight.shape[0]
    hidden_rows = second_feed_weight.shape[0]
    hidden = shards * hidden_rows
    out_rows = attention_output_weight.shape[0]
    whole_heads = out_rows == HD and heads == shards

    x_own, g_own = block_input[0], cotangent[0]
    x_all = gather_tokens(x_own, groups)
    g_all = gather_tokens(g_own, groups)

    wqkv = to_columns(query_key_value_weight.reshape(rows, 3 * heads, groups, HD), groups)
    wqkv = lax.all_gather(wqkv, "fsdp", axis=0, tiled=True)
    if whole_heads:
        wout = lax.all_gather(attention_output_weight, "fsdp", axis=0, tiled=True)
    else:
        wout = lax.all_gather(attention_output_weight, BOTH, axis=0, tiled=True)
        wout = take(wout.reshape(heads, groups, HD, width), me, 1).reshape(heads * HD, width)
    wfc1 = to_columns(first_feed_weight.reshape(rows, shards, groups, hidden_rows), groups)
    wfc1 = lax.all_gather(wfc1, "fsdp", axis=0, tiled=True)
    wfc2 = lax.all_gather(second_feed_weight, "fsdp", axis=0, tiled=True)

    vectors = (
        ln_gain,
        norm_layer_bias,
        query_key_value_bias,
        attention_output_bias,
        first_feed_bias,
        second_feed_bias,
    )
    small = gather_small(jnp.concatenate(vectors), size).astype(f32)
    pieces, at = [], 0
    for vector in vectors:
        pieces.append(small[:, at : at + vector.shape[0]].reshape(-1))
        at += vector.shape[0]
    gain, shift, bqkv, bout, bfc1, bfc2 = pieces
    bqkv = take(bqkv.reshape(3, heads, groups, HD), me, 2).reshape(-1)
    bfc1 = take(bfc1.reshape(shards, groups, hidden_rows), me, 1).reshape(-1)

    normed_all = (normalise(x_all.astype(f32))[0] * gain + shift).astype(bf16)
    freqs = 10000.0 ** (-2.0 * jnp.arange(ROT // 2).astype(f32) / ROT)
    angles = freqs[:, None] * jnp.arange(length).astype(f32)[None, :]
    cosine, sine = jnp.cos(angles), jnp.sin(angles)
    projected = dot(wqkv, normed_all, 0, 1) + bqkv[:, None]
    projected = projected.reshape(3, heads, HD, length)
    turned = rotate(projected[:2], cosine, sine)
    qkv = jnp.concatenate([turned, projected[2:]], 0).astype(bf16).reshape(3 * heads * HD, length)
    attn, lse = attend_forward(qkv, heads)
    up_pre = dot(wfc1, normed_all, 0, 1) + bfc1[:, None]
    up_value, gelu_pull = jax.vjp(gelu_tanh, up_pre)
    up = up_value.astype(bf16)
    mixed = dot(attn, wout, 0, 0) + dot(up, wfc2, 0, 0)
    mixed = scatter_tokens(mixed.astype(bf16), groups)
    block_output = (x_own.astype(f32) + mixed + bout + bfc2).astype(bf16)

    d_attn = dot(wout, g_all, 1, 1).astype(bf16)
    d_qkv = attend_backward(qkv, attn, d_attn, lse, heads).astype(f32)
    d_turned = rotate(d_qkv[:2], cosine, -sine)
    d_proj = jnp.concatenate([d_turned, d_qkv[2:]], 0).astype(bf16).reshape(3 * heads * HD, length)
    (d_pre,) = gelu_pull(dot(wfc2, g_all, 1, 1))
    d_pre = d_pre.astype(bf16)
    d_normed = dot(d_proj, wqkv, 0, 1) + dot(d_pre, wfc1, 0, 1)
    d_normed = scatter_tokens(d_normed.astype(bf16), groups)
    xhat, inverse = normalise(x_own.astype(f32))
    e = d_normed * gain
    d_x = (e - jnp.mean(e, -1, keepdims=True) - xhat * jnp.mean(e * xhat, -1, keepdims=True)) * inverse
    grad_input = g_own.astype(f32) + d_x

    term_wqkv = dot(normed_all, d_proj, 0, 1).astype(bf16)
    term_wout = dot(attn, g_all, 1, 0)
    term_wfc1 = dot(normed_all, d_pre, 0, 1).astype(bf16)
    term_wfc2 = dot(up, g_all, 1, 0).astype(bf16)
    grad_wqkv = lax.psum_scatter(term_wqkv, "fsdp", scatter_dimension=0, tiled=True)
    grad_wqkv = to_rows(grad_wqkv, groups, 3 * heads).reshape(rows, 3 * H * HD).astype(f32)
    if whole_heads:
        grad_wout = lax.psum_scatter(term_wout.astype(bf16), "fsdp", scatter_dimension=0, tiled=True).astype(f32)
    else:
        mask = (jnp.arange(groups) == me).astype(f32)
        spread = term_wout.reshape(heads, 1, HD, width) * mask[None, :, None, None]
        spread = spread.astype(bf16).reshape(H * HD, width)
        grad_wout = lax.psum_scatter(spread, BOTH, scatter_dimension=0, tiled=True).astype(f32)
    grad_wfc1 = lax.psum_scatter(term_wfc1, "fsdp", scatter_dimension=0, tiled=True)
    grad_wfc1 = to_rows(grad_wfc1, groups, shards).reshape(rows, -1).astype(f32)
    grad_wfc2 = lax.psum_scatter(term_wfc2, "fsdp", scatter_dimension=0, tiled=True).astype(f32)

    here = (jnp.arange(groups) == me).astype(f32)
    term_bqkv = jnp.sum(d_proj.astype(f32), 1).reshape(3 * heads, 1, HD) * here[None, :, None]
    term_bqkv = term_bqkv.reshape(-1)
    term_bfc1 = (jnp.sum(d_pre.astype(f32), 1).reshape(shards, 1, hidden_rows) * here[None, :, None]).reshape(-1)
    terms = (
        jnp.sum(d_normed * xhat, 0),
        jnp.sum(d_normed, 0),
        term_bqkv[: 2 * H * HD],
        term_bqkv[2 * H * HD :],
        jnp.sum(g_own.astype(f32), 0),
        term_bfc1,
    )
    summed = scatter_small(jnp.concatenate([t.reshape(size, -1) for t in terms], 1), size)
    vector_grads, at = [], 0
    for term in terms:
        count = term.shape[0] // size
        vector_grads.append(summed[at : at + count])
        at += count
    grad_gain, grad_shift, grad_bqk, grad_bv, grad_bout, grad_bfc1 = vector_grads
    return (
        block_output[None],
        grad_input[None],
        grad_gain,
        grad_shift,
        grad_wqkv,
        grad_bqk,
        grad_bv,
        grad_wout,
        grad_bout,
        grad_wfc1,
        grad_bfc1,
        grad_wfc2,
        grad_bout,
    )


def solution(mesh):
    tokens, split = P("fsdp", "seq", None), P(BOTH)
    return jax.shard_map(
        local,
        mesh=mesh,
        in_specs=(tokens, *([split] * 10), tokens),
        out_specs=(tokens, tokens, *([split] * 11)),
        check_vma=False,
    )
```

time: 3140 us -> 557 us (0.18)
  waiting for transfers between devices: 2280 us -> 92.4 us
  matrix products: 455 us -> 149 us
  blocking collectives: 126 us -> 37.2 us
  Pallas kernels: 0 us -> 43.3 us
    reduce_scatter x4, waiting for transfers between devices: 2040 us -> 10.8 us  [the longest x1 10.8 us: local(): lax.psum_scatter(term_wfc2, 'fsdp', scatter_dimension=0, tiled=True)]
    dot_general x32 -> x12, matrix products: 366 us -> 149 us  [dot(): lax.dot_general(a, b, (((ca,), (cb,)), ((), ())), preferred_element_type=...]
    all_gather x4, waiting for transfers between devices: 167 us -> 0.01 us  [the longest x1 0.01 us: local(): wout = lax.all_gather(attention_output_weight, 'fsdp', axis=0, tiled=True)]
    sub x8 -> x0, matrix products: 89 us -> none  [block_probs(): expo = jnp.exp(score_matrix - row_max)]
    all_gather x1 -> x0, blocking collectives: 82 us -> none  [local(): lax.all_gather(first_feed_bias, ('fsdp', 'seq'), axis=0, tiled=True)]
    ppermute x0 -> x28, waiting for transfers between devices: none -> 80.8 us  [the longest x26 74.2 us: swap(): return lax.ppermute(value, axes, [(i, i ^ bit) for i in range(size)])]
    all_to_all x4 -> x2, waiting for transfers between devices: 65 us -> 0.01 us  [to_rows(): got = lax.all_to_all(grads, 'seq', split_axis=0, concat_axis=0, tiled=True)]
    unnamed x1 -> x0, blocking collectives: 43.7 us -> none
  transfers between devices with their start and end apart: 13 -> 38, of which waited for: 8 -> 11; matrix products, arithmetic and copies ran while one was open for 20% -> 55% of each run, Pallas kernels for 0% -> 8%
where the time goes in v1:
time: 557 us; the launch traced here: 552 us
  matrix products  149 us (27%)
  local copies, waits for them, and re-layouts  114 us (20%)
  waiting for transfers between devices  92.4 us (17%)
  other arithmetic  64.6 us (12%)
  Pallas kernels  43.3 us (8%)
  blocking collectives  37.2 us (7%)
  starting transfers between devices  35.6 us (6%)
  between operations  15.4 us (3%)
    dot_general x12, matrix products, dot(): lax.dot_general(a, b, (((ca,), (cb,)), ((), ())), preferred_element_type=...  149 us
    ppermute x26, waiting for transfers between devices, swap(): return lax.ppermute(value, axes, [(i, i ^ bit) for i in range(size)])  74.2 us
    all_to_all x2, blocking collectives, to_columns(): return lax.all_to_all(sent, 'seq', split_axis=0, concat_axis=0, tiled=True)  37.2 us
    pallas_call x1, Pallas kernels, attend_backward(): pl.pallas_call(functools.partial(backward_kernel, block), grid=(heads,),...  27.9 us
    ppermute x26, starting transfers between devices, swap(): return lax.ppermute(value, axes, [(i, i ^ bit) for i in range(size)])  23.8 us
    pallas_call x1, Pallas kernels, attend_forward(): pl.pallas_call(functools.partial(forward_kernel, block), grid=(heads,), i...  15.3 us
    convert_element_type x2, other arithmetic, local(): normed_all = (normalise(x_all.astype(f32))[0] * gain + shift).astype(bf16)  14.4 us
    unnamed x101, local copies, waits for them, and re-layouts  13.2 us
  transfers between devices with their start and end apart: 38, of which 11 were waited for; matrix products, arithmetic and copies ran while one was open for 55% of the time, Pallas kernels for 8%

profile of v1, /device:TPU:0, one launch (start us, length us, event | category | flops | bytes accessed | tf_op | source)
XLA Modules:
  0.0 552.0 jit_solution(4636289449680316883)
XLA Ops:
  13.7 17.6 %all_to_all.42 = bf16[8,64,768]{2,1,0:T(8,128)(2,1)} all-to-all(bf16[8,64,768]{2,1,0:T(8,128)(2,1)S(1)} %all_to_all.28), channel_id=1, replica_groups=mesh['fsdp'=4,'seq'=8] {'seq'}, dimensions={0} | all-to-all | bytes 1572864 | tf_op jit(solution)/shard_map/all_to_all | solution.py:246
  35.7 19.6 %all_to_all.43 = bf16[8,64,1024]{2,1,0:T(8,128)(2,1)} all-to-all(bf16[8,64,1024]{2,1,0:T(8,128)(2,1)} %all_to_all.31), channel_id=1, replica_groups=mesh['fsdp'=4,'seq'=8] {'seq'}, dimensions={0} | all-to-all | bytes 2097152 | tf_op jit(solution)/shard_map/all_to_all | solution.py:246
  70.8 31.5 %collective-permute-done.5 = bf16[2,704]{1,0:T(2,128)(2,1)} collective-permute-done((bf16[2,704]{1,0:T(2,128)(2,1)S(1)}, bf16[2,704]{1,0:T(2,128)(2,1)}, u32[]{:S(2)}, u32[]{:S(2)}) %collective-permute-start.5) | collective-permute-done | bytes 2848 | tf_op jit(solution)/shard_map/ppermute | solution.py:170
  125.5 6.2 %collective-permute-done.2 = bf16[256,2048]{1,0:T(8,128)(2,1)S(1)} collective-permute-done((bf16[256,2048]{1,0:T(8,128)(2,1)S(1)}, bf16[256,2048]{1,0:T(8,128)(2,1)S(1)}, u32[]{:S(2)}, u32[]{:S(2)}) %collective-permute-start.2) | collective-permute-done | bytes 1048608 | tf_op jit(solution)/shard_map/ppermute | solution.py:206
  170.9 5.7 %fusion.3 = bf16[2048,2048]{1,0:T(8,128)(2,1)} fusion(bf16[4,2,256,2048]{3,2,1,0:T(8,128)(2,1)S(1)} %bitcast_dynamic-update-slice_fusion.3, f32[2048]{0:T(1024)S(1)} %add.261, f32[2048]{0:T(1024)S(1)} %mul.316, f32[2048]{0:T(1024)S(1)} %bitcast.249, f32[2048]{0:T(1024)S(1)} %bitcast.250), kind=kLoop, calls=%fused_computation.4 | loop fusion | flops 25165824 | bytes 16809984 | tf_op jit(solution)/shard_map/convert_element_type | solution.py:313
  176.6 10.5 %add_bitcast_fusion = f32[768,2048]{1,0:T(8,128)S(1)} fusion(f32[768]{0:T(1024)S(1)} %copy-done.34, bf16[2048,2048]{1,0:T(8,128)(2,1)} %fusion.3, bf16[2048,768]{1,0:T(8,128)(2,1)} %all-gather.5.cloned.1.call-done), kind=kOutput, calls=%fused_computation.35 | convolution fusion | flops 6444023808 | bytes 17828864 | tf_op jit(solution)/shard_map/dot_general | solution.py:20
  188.3 15.3 %attend_forward.1 = (bf16[256,2048]{1,0:T(8,128)(2,1)S(1)}, f32[4,1,2048]{2,1,0:T(1,128)S(1)}) custom-call(bf16[768,2048]{1,0:T(8,128)(2,1)S(1)} %bitcast.215, bf16[768,2048]{1,0:T(8,128)(2,1)S(1)} %bitcast.216, bf16[768,2048]{1,0:T(8,128)(2,1)S(1)} %bitcast.217), custom_call_target="tpu_custom_call" | custom-call | flops 17179869184 | bytes 4194304 | tf_op jit(solution)/shard_map/attend_forward/pallas_call | solution.py:65
  209.4 6.5 %fusion.16.g_ref = bf16[256,2048]{1,0:T(8,128)(2,1)S(1)} fusion(bf16[2048,2048]{1,0:T(8,128)(2,1)} %bitcast.40, bf16[256,2048]{1,0:T(8,128)(2,1)} %all-gather.7.cloned.1.call-done), kind=kOutput, calls=%fused_computation.55 | convolution fusion | flops 2148007936 | bytes 10485760 | tf_op jit(solution)/shard_map/dot_general | solution.py:20
  215.9 27.9 %attend_backward.1 = bf16[3,4,64,2048]{3,2,1,0:T(8,128)(2,1)S(1)} custom-call(bf16[768,2048]{1,0:T(8,128)(2,1)} %bitcast.218, bf16[768,2048]{1,0:T(8,128)(2,1)} %bitcast.219, bf16[768,2048]{1,0:T(8,128)(2,1)} %bitcast.220, bf16[256,2048]{1,0:T(8,128)(2,1)S(1)} %copy-done.2, bf16[256,2048]{1,0:T(8,128)(2,1)S(1)} %fusion.16.g_ref, ...), custom_call_target="tpu_custom_call" | custom-call | flops 34359738368 | bytes 8388608 | tf_op jit(solution)/shard_map/attend_backward/pallas_call | solution.py:127
  247.2 6.8 %convolution_convert_fusion.3 = bf16[256,2048]{1,0:T(8,128)(2,1)} fusion(bf16[256,2048]{1,0:T(8,128)(2,1)S(1)} %copy-done.2, bf16[2048,2048]{1,0:T(8,128)(2,1)} %bitcast.40), kind=kOutput, calls=%fused_computation.51 | convolution fusion | flops 2148007936 | bytes 10485760 | tf_op jit(solution)/shard_map/dot_general | solution.py:20
  254.0 8.7 %add_convert_fusion = bf16[4,2,256,2048]{3,2,1,0:T(8,128)(2,1)} fusion(bf16[4,2,256,2048]{3,2,1,0:T(8,128)(2,1)} %copy-done.4, f32[2048]{0:T(1024)S(1)} %add.261, f32[2048]{0:T(1024)S(1)} %mul.316, f32[4,2,256]{2,1,0:T(2,128)S(1)} %copy-done.27, f32[4,2,256]{2,1,0:T(2,128)S(1)} %copy-done.23), kind=kLoop, calls=%fused_computation.5 | loop fusion | flops 25165824 | bytes 16809984 | tf_op jit(solution)/shard_map/convert_element_type | solution.py:313
  263.5 10.5 %convolution_convert_fusion.2 = bf16[2048,768]{1,0:T(8,128)(2,1)} fusion(bf16[2048,2048]{1,0:T(8,128)(2,1)} %bitcast.235, bf16[768,2048]{1,0:T(8,128)(2,1)S(1)} %bitcast.242), kind=kOutput, calls=%fused_computation.45 | convolution fusion | flops 6444023808 | bytes 14680064 | tf_op jit(solution)/shard_map/dot_general | solution.py:20
  274.1 12.2 %fusion.52 = f32[2048,2048]{1,0:T(8,128)} fusion(bf16[768,2048]{1,0:T(8,128)(2,1)S(1)} %bitcast.243, bf16[2048,768]{1,0:T(8,128)(2,1)} %all-gather.5.cloned.1.call-done), kind=kOutput, calls=%fused_computation.178 | convolution fusion | flops 6442450944 | bytes 23068672 | tf_op jit(solution)/shard_map/dot_general | solution.py:20
  286.2 14.4 %fusion.51 = f32[2048,1024]{1,0:T(8,128)} fusion(bf16[2048,2048]{1,0:T(8,128)(2,1)} %fusion.3, bf16[2048,1024]{1,0:T(8,128)(2,1)} %all-gather.9.cloned.1.call-done), kind=kOutput, calls=%fused_computation.177 | convolution fusion | flops 8589934592 | bytes 20971520 | tf_op jit(solution)/shard_map/dot_general | solution.py:20
  300.6 20.1 %convert_reduce_fusion.1 = (f32[1024]{0:T(1024)S(1)}, bf16[1024,2048]{0,1:T(8,128)(2,1)S(1)}) fusion(bf16[2048,2048]{1,0:T(8,128)(2,1)} %bitcast.40, bf16[1024,2048]{1,0:T(8,128)(2,1)} %all-gather.11.cloned.1.call-done, f32[2048,1024]{1,0:T(8,128)} %fusion.51, f32[1024]{0:T(1024)S(1)} %bitcast.251), kind=kOutput, calls=%fused_computation.31 | convolution fusion | flops 8646556672 | bytes 25174016 | tf_op jit(solution)/shard_map/dot_general | solution.py:20
  322.8 12.9 %convolution_convert_fusion.1 = bf16[2048,1024]{1,0:T(8,128)(2,1)} fusion(bf16[2048,2048]{1,0:T(8,128)(2,1)} %fusion.3, bf16[1024,2048]{0,1:T(8,128)(2,1)S(1)} %get-tuple-element.61), kind=kOutput, calls=%fused_computation.44 | convolution fusion | flops 8592031744 | bytes 16777216 | tf_op jit(solution)/shard_map/dot_general | solution.py:20
  335.7 14.9 %add_convert_fusion.1 = bf16[2048,2048]{1,0:T(8,128)(2,1)S(1)} fusion(f32[2048,2048]{1,0:T(8,128)} %fusion.52, bf16[1024,2048]{0,1:T(8,128)(2,1)} %copy-done.45, bf16[2048,1024]{1,0:T(8,128)(2,1)} %all-gather.9.cloned.1.call-done), kind=kOutput, calls=%fused_computation.6 | convolution fusion | flops 8598323200 | bytes 33554432 | tf_op jit(solution)/shard_map/dot_general | solution.py:20
  357.3 15.4 %fusion.47 = f32[2048,2048]{1,0:T(8,128)} fusion(bf16[1024,2048]{1,0:T(8,128)(2,1)S(1)} %copy-done.44, f32[2048,1024]{1,0:T(8,128)} %fusion.51, f32[1024]{0:T(1024)S(1)} %bitcast.252), kind=kOutput, calls=%fused_computation.173 | convolution fusion | flops 8610906112 | bytes 29364224 | tf_op jit(solution)/shard_map/dot_general | solution.py:20
  372.7 8.3 %add_convert_fusion.2 = bf16[2048,2048]{1,0:T(8,128)(2,1)S(1)} fusion(f32[2048,2048]{1,0:T(8,128)} %fusion.47, bf16[256,2048]{1,0:T(8,128)(2,1)S(1)} %copy-done.3, bf16[256,2048]{1,0:T(8,128)(2,1)S(1)} %copy-done.18), kind=kOutput, calls=%fused_computation.7 | convolution fusion | flops 2155872256 | bytes 27262976 | tf_op jit(solution)/shard_map/dot_general | solution.py:20
  386.5 16.7 %convolution_convert_fusion = bf16[1024,2048]{1,0:T(8,128)(2,1)} fusion(bf16[2048,2048]{1,0:T(8,128)(2,1)} %bitcast.40, f32[2048,1024]{1,0:T(8,128)} %fusion.51, f32[1024]{0:T(1024)S(1)} %bitcast.253), kind=kOutput, calls=%fused_computation.43 | convolution fusion | flops 8613003264 | bytes 20975616 | tf_op jit(solution)/shard_map/dot_general | solution.py:20
  433.9 8.7 %collective-permute-done.19 = bf16[2,256,1024]{2,1,0:T(8,128)(2,1)} collective-permute-done((bf16[2,256,1024]{2,1,0:T(8,128)(2,1)}, bf16[2,256,1024]{2,1,0:T(8,128)(2,1)}, u32[]{:S(2)}, u32[]{:S(2)}) %collective-permute-start.19) | collective-permute-done | bytes 1048608 | tf_op jit(solution)/shard_map/ppermute | solution.py:170
  448.4 16.8 %collective-permute-done.10 = bf16[2,256,1024]{2,1,0:T(8,128)(2,1)} collective-permute-done((bf16[2,256,1024]{2,1,0:T(8,128)(2,1)S(1)}, bf16[2,256,1024]{2,1,0:T(8,128)(2,1)}, u32[]{:S(2)}, u32[]{:S(2)}) %collective-permute-start.10) | collective-permute-done | bytes 1048608 | tf_op jit(solution)/shard_map/ppermute | solution.py:170
  470.0 7.3 %collective-permute-done.20 = bf16[256,1024]{1,0:T(8,128)(2,1)S(1)} collective-permute-done((bf16[256,1024]{1,0:T(8,128)(2,1)S(1)}, bf16[256,1024]{1,0:T(8,128)(2,1)S(1)}, u32[]{:S(2)}, u32[]{:S(2)}) %collective-permute-start.20) | collective-permute-done | bytes 524320 | tf_op jit(solution)/shard_map/ppermute | solution.py:170
  525.1 10.8 %reduce-scatter.11.cloned.1.call-done = bf16[256,2048]{1,0:T(8,128)(2,1)} async-done(((bf16[1024,2048]{1,0:T(8,128)(2,1)}), bf16[256,2048]{1,0:T(8,128)(2,1)}) %reduce-scatter.11.cloned.1.call-update) | async-done | bytes 1048592 | tf_op jit(solution)/shard_map/reduce_scatter | solution.py:357
  (309 shorter events, 211.3 us)
Async XLA Ops:
  7.2 169.4 %all-gather.5.cloned.1.call-start = ((), (), s32[]{:S(2)}) async-start(), calls=%async_computation.8 | async-start | bytes 3932160 | tf_op jit(solution)/shard_map/all_gather | solution.py:286
  31.3 178.0 %all-gather.7.cloned.1.call-start = ((), (), s32[]{:S(2)}) async-start(), calls=%async_computation.9 | async-start | bytes 1310720 | tf_op jit(solution)/shard_map/all_gather | solution.py:288
  32.1 254.2 %all-gather.9.cloned.1.call-start = ((), (), s32[]{:S(2)}) async-start(), calls=%async_computation.10 | async-start | bytes 5242880 | tf_op jit(solution)/shard_map/all_gather | solution.py:293
  55.3 245.3 %all-gather.11.cloned.1.call-start = ((), (), s32[]{:S(2)}) async-start(), calls=%async_computation.11 | async-start | bytes 5242880 | tf_op jit(solution)/shard_map/all_gather | solution.py:294
  55.4 60.1 %collective-permute-start = (bf16[256,2048]{1,0:T(8,128)(2,1)S(1)}, bf16[256,2048]{1,0:T(8,128)(2,1)}, u32[]{:S(2)}, u32[]{:S(2)}) collective-permute-start(bf16[256,2048]{1,0:T(8,128)(2,1)S(1)} %bitcast.225), channel_id=1, source_target_pairs={{0,2},{1,3},{2,0},{3,1},{4,6},{5,7},{6,4},{7,5},{8,10},{9,11},{10,... | collective-permute-start | bytes 3145736 | tf_op jit(solution)/shard_map/ppermute | solution.py:170
  56.0 59.5 %collective-permute-start.1 = (bf16[256,2048]{1,0:T(8,128)(2,1)S(1)}, bf16[256,2048]{1,0:T(8,128)(2,1)}, u32[]{:S(2)}, u32[]{:S(2)}) collective-permute-start(bf16[256,2048]{1,0:T(8,128)(2,1)S(1)} %bitcast.226), channel_id=1, source_target_pairs={{0,4},{1,5},{2,6},{3,7},{4,0},{5,1},{6,2},{7,3},{8,12},{9,13},{10,... | collective-permute-start | bytes 3145736 | tf_op jit(solution)/shard_map/ppermute | solution.py:170
  56.6 77.0 %collective-permute-start.14 = (bf16[256,2048]{1,0:T(8,128)(2,1)S(1)}, bf16[256,2048]{1,0:T(8,128)(2,1)S(1)}, u32[]{:S(2)}, u32[]{:S(2)}) collective-permute-start(bf16[256,2048]{1,0:T(8,128)(2,1)S(1)} %bitcast.230), channel_id=1, source_target_pairs={{0,2},{1,3},{2,0},{3,1},{4,6},{5,7},{6,4},{7,5},{8,10},{9,11},{10,... | collective-permute-start | bytes 3145736 | tf_op jit(solution)/shard_map/ppermute | solution.py:170
  58.0 75.6 %collective-permute-start.15 = (bf16[256,2048]{1,0:T(8,128)(2,1)S(1)}, bf16[256,2048]{1,0:T(8,128)(2,1)}, u32[]{:S(2)}, u32[]{:S(2)}) collective-permute-start(bf16[256,2048]{1,0:T(8,128)(2,1)S(1)} %bitcast.231), channel_id=1, source_target_pairs={{0,4},{1,5},{2,6},{3,7},{4,0},{5,1},{6,2},{7,3},{8,12},{9,13},{10,... | collective-permute-start | bytes 3145736 | tf_op jit(solution)/shard_map/ppermute | solution.py:170
  60.2 368.2 %reduce-scatter.7.cloned.1.call-start = ((), (), s32[]{:S(2)}) async-start(), calls=%async_computation.13 | async-start | bytes 1310720 | tf_op jit(solution)/shard_map/reduce_scatter | solution.py:349
  69.6 32.7 %collective-permute-start.5 = (bf16[2,704]{1,0:T(2,128)(2,1)S(1)}, bf16[2,704]{1,0:T(2,128)(2,1)}, u32[]{:S(2)}, u32[]{:S(2)}) collective-permute-start(bf16[2,704]{1,0:T(2,128)(2,1)S(1)} %pad_maximum_fusion.5), channel_id=1, source_target_pairs={{0,2},{1,3},{2,0},{3,1},{4,6},{5,7},{6,4},{7,5},{8,10},{9,11},{10,... | collective-permute-start | bytes 8456 | tf_op jit(solution)/shard_map/ppermute | solution.py:170
  132.8 31.1 %collective-permute-start.3 = (bf16[4,256,2048]{2,1,0:T(8,128)(2,1)}, bf16[4,256,2048]{2,1,0:T(8,128)(2,1)}, u32[]{:S(2)}, u32[]{:S(2)}) collective-permute-start(bf16[4,256,2048]{2,1,0:T(8,128)(2,1)} %bitcast_dynamic-update-slice_fusion.7), channel_id=1, source_target_pairs={{0,1},{1,0},{2,3},{3,2},{4,5},{5,4},{6,7},{7,6},{8,9},{9,8},{10,11... | collective-permute-start | bytes 12582920 | tf_op jit(solution)/shard_map/ppermute | solution.py:170
  150.9 53.6 %collective-permute-start.17 = (bf16[4,256,2048]{2,1,0:T(8,128)(2,1)}, bf16[4,256,2048]{2,1,0:T(8,128)(2,1)}, u32[]{:S(2)}, u32[]{:S(2)}) collective-permute-start(bf16[4,256,2048]{2,1,0:T(8,128)(2,1)} %bitcast_dynamic-update-slice_fusion.4), channel_id=1, source_target_pairs={{0,1},{1,0},{2,3},{3,2},{4,5},{5,4},{6,7},{7,6},{8,9},{9,8},{10,11... | collective-permute-start | bytes 12582920 | tf_op jit(solution)/shard_map/ppermute | solution.py:170
  262.7 221.9 %reduce-scatter.5.cloned.1.call-start = ((), (), s32[]{:S(2)}) async-start(), calls=%async_computation.12 | async-start | bytes 3932160 | tf_op jit(solution)/shard_map/reduce_scatter | solution.py:346
  274.0 230.9 %reduce-scatter.9.cloned.1.call-start = ((), (), s32[]{:S(2)}) async-start(), calls=%async_computation.14 | async-start | bytes 5242880 | tf_op jit(solution)/shard_map/reduce_scatter | solution.py:355
  335.7 200.2 %reduce-scatter.11.cloned.1.call-start = ((), (), s32[]{:S(2)}) async-start(), calls=%async_computation.15 | async-start | bytes 5242880 | tf_op jit(solution)/shard_map/reduce_scatter | solution.py:357
  356.1 47.1 %collective-permute-start.18 = (bf16[2,2,256,2048]{3,2,0,1:T(8,128)(2,1)}, bf16[2,2,256,2048]{3,2,0,1:T(8,128)(2,1)}, u32[]{:S(2)}, u32[]{:S(2)}) collective-permute-start(bf16[2,2,256,2048]{3,2,0,1:T(8,128)(2,1)} %bitcast.212), channel_id=1, source_target_pairs={{0,1},{1,0},{2,3},{3,2},{4,5},{5,4},{6,7},{7,6},{8,9},{9,8},{10,11... | collective-permute-start | bytes 12582920 | tf_op jit(solution)/shard_map/ppermute | solution.py:170
  385.9 32.0 %collective-permute-start.9 = (bf16[2,2,256,2048]{3,2,1,0:T(8,128)(2,1)}, bf16[2,2,256,2048]{3,2,1,0:T(8,128)(2,1)}, u32[]{:S(2)}, u32[]{:S(2)}) collective-permute-start(bf16[2,2,256,2048]{3,2,1,0:T(8,128)(2,1)} %dynamic-slice_bitcast_fusion), channel_id=1, source_target_pairs={{0,1},{1,0},{2,3},{3,2},{4,5},{5,4},{6,7},{7,6},{8,9},{9,8},{10,11... | collective-permute-start | bytes 12582920 | tf_op jit(solution)/shard_map/ppermute | solution.py:170
  416.3 26.3 %collective-permute-start.19 = (bf16[2,256,1024]{2,1,0:T(8,128)(2,1)}, bf16[2,256,1024]{2,1,0:T(8,128)(2,1)}, u32[]{:S(2)}, u32[]{:S(2)}) collective-permute-start(bf16[2,256,1024]{2,1,0:T(8,128)(2,1)} %fusion.33), channel_id=1, source_target_pairs={{0,2},{1,3},{2,0},{3,1},{4,6},{5,7},{6,4},{7,5},{8,10},{9,11},{10,... | collective-permute-start | bytes 3145736 | tf_op jit(solution)/shard_map/ppermute | solution.py:170
  417.6 27.7 %collective-permute-start.21 = (bf16[2,256,1024]{2,1,0:T(8,128)(2,1)S(1)}, bf16[2,256,1024]{2,1,0:T(8,128)(2,1)}, u32[]{:S(2)}, u32[]{:S(2)}) collective-permute-start(bf16[2,256,1024]{2,1,0:T(8,128)(2,1)S(1)} %fusion.34), channel_id=1, source_target_pairs={{0,4},{1,5},{2,6},{3,7},{4,0},{5,1},{6,2},{7,3},{8,12},{9,13},{10,... | collective-permute-start | bytes 3145736 | tf_op jit(solution)/shard_map/ppermute | solution.py:170
  427.4 37.7 %collective-permute-start.10 = (bf16[2,256,1024]{2,1,0:T(8,128)(2,1)S(1)}, bf16[2,256,1024]{2,1,0:T(8,128)(2,1)}, u32[]{:S(2)}, u32[]{:S(2)}) collective-permute-start(bf16[2,256,1024]{2,1,0:T(8,128)(2,1)S(1)} %fusion.31), channel_id=1, source_target_pairs={{0,2},{1,3},{2,0},{3,1},{4,6},{5,7},{6,4},{7,5},{8,10},{9,11},{10,... | collective-permute-start | bytes 3145736 | tf_op jit(solution)/shard_map/ppermute | solution.py:170
  432.1 36.3 %collective-permute-start.12 = (bf16[2,256,1024]{2,1,0:T(8,128)(2,1)S(1)}, bf16[2,256,1024]{2,1,0:T(8,128)(2,1)S(1)}, u32[]{:S(2)}, u32[]{:S(2)}) collective-permute-start(bf16[2,256,1024]{2,1,0:T(8,128)(2,1)S(1)} %fusion.32), channel_id=1, source_target_pairs={{0,4},{1,5},{2,6},{3,7},{4,0},{5,1},{6,2},{7,3},{8,12},{9,13},{10,... | collective-permute-start | bytes 3145736 | tf_op jit(solution)/shard_map/ppermute | solution.py:170
  445.0 32.3 %collective-permute-start.20 = (bf16[256,1024]{1,0:T(8,128)(2,1)S(1)}, bf16[256,1024]{1,0:T(8,128)(2,1)S(1)}, u32[]{:S(2)}, u32[]{:S(2)}) collective-permute-start(bf16[256,1024]{1,0:T(8,128)(2,1)S(1)} %fusion.40), channel_id=1, source_target_pairs={{0,4},{1,5},{2,6},{3,7},{4,0},{5,1},{6,2},{7,3},{8,12},{9,13},{10,... | collective-permute-start | bytes 1572872 | tf_op jit(solution)/shard_map/ppermute | solution.py:170
  447.2 30.3 %collective-permute-start.22 = (bf16[256,1024]{1,0:T(8,128)(2,1)S(1)}, bf16[256,1024]{1,0:T(8,128)(2,1)S(1)}, u32[]{:S(2)}, u32[]{:S(2)}) collective-permute-start(bf16[256,1024]{1,0:T(8,128)(2,1)S(1)} %fusion.41), channel_id=1, source_target_pairs={{0,2},{1,3},{2,0},{3,1},{4,6},{5,7},{6,4},{7,5},{8,10},{9,11},{10,... | collective-permute-start | bytes 1572872 | tf_op jit(solution)/shard_map/ppermute | solution.py:170
  504.9 33.7 %all-to-all-start.3 = ((bf16[8,64,1024]{2,1,0:T(8,128)(2,1)}), bf16[8,64,1024]{2,1,0:T(8,128)(2,1)}, u32[]{:S(2)}, u32[]{:S(2)}) async-start(bf16[8,64,1024]{2,1,0:T(8,128)(2,1)} %bitcast.247), calls=%async_computation.6 | async-start | bytes 2097152 | tf_op jit(solution)/shard_map/all_to_all | solution.py:251
  (63 other events, 862.3 us)
Sparse Core Ops, SparseCore 0:
  31.4 62.8 all-gather.4
  95.9 27.2 all-gather.6
  124.8 80.5 all-gather.8
  206.8 79.2 all-gather.10
  288.8 25.6 reduce-scatter.6
  316.8 58.8 reduce-scatter.4
  378.2 76.7 reduce-scatter.8
  457.3 78.5 reduce-scatter.10

commit v2 on v1

v2 whole, which is shorter than its diff:
```python
import functools

import jax
import jax.numpy as jnp
from jax import lax
from jax.experimental import pallas as pl
from jax.experimental.pallas import tpu as pltpu
from jax.sharding import PartitionSpec as P

H = 32
HD = 64
ROT = 32
EPSILON = 1e-05
BOTH = ("fsdp", "seq")
f32 = jnp.float32
bf16 = jnp.bfloat16


def dot(a, b, ca, cb):
    return lax.dot_general(a, b, (((ca,), (cb,)), ((), ())), preferred_element_type=f32)


def causal(tile):
    keys = lax.broadcasted_iota(jnp.int32, tile.shape, 0)
    queries = lax.broadcasted_iota(jnp.int32, tile.shape, 1)
    return jnp.where(queries >= keys, tile, -1e30)


def forward_kernel(block, q_ref, k_ref, v_ref, cos_ref, sin_ref, *refs):
    o_ref, lse_ref, qkv_ref, kn_ref = refs[-4:]
    blocks = q_ref.shape[1] // block
    qkv_ref[0, 0] = rotate(q_ref[...], cos_ref[...], sin_ref[...]).astype(bf16)
    turned = rotate(k_ref[...], cos_ref[...], sin_ref[...]).astype(bf16)
    qkv_ref[1, 0] = turned
    kn_ref[...] = turned.T
    qkv_ref[2, 0] = v_ref[...].astype(bf16)
    for i in range(blocks):
        rows = pl.ds(i * block, block)
        q = qkv_ref[0, 0, :, rows] * jnp.asarray(HD**-0.5, bf16)
        best = total = acc = None
        for j in range(i, -1, -1):
            cols = pl.ds(j * block, block)
            s = dot(kn_ref[cols, :], q, 1, 0)
            if j == i:
                s = causal(s)
            top = jnp.max(s, 0, keepdims=True)
            v = qkv_ref[2, 0, :, cols]
            if best is None:
                best = top
                p = jnp.exp(s - best)
                total = jnp.sum(p, 0, keepdims=True)
                acc = dot(v, p.astype(bf16), 1, 0)
            else:
                new = jnp.maximum(best, top)
                fade = jnp.exp(best - new)
                p = jnp.exp(s - new)
                total = total * fade + jnp.sum(p, 0, keepdims=True)
                acc = acc * fade + dot(v, p.astype(bf16), 1, 0)
                best = new
        o_ref[:, rows] = (acc / total).astype(bf16)
        lse_ref[0, :, rows] = best + jnp.log(total)


def attend_forward(projected, cosine, sine, heads, *others):
    length = projected.shape[1]
    block = length // 2

    def spec(part):
        return pl.BlockSpec((HD, length), lambda h: (part * heads + h, 0))

    table = pl.BlockSpec((ROT // 2, length), lambda h: (0, 0))
    return pl.pallas_call(
        functools.partial(forward_kernel, block),
        grid=(heads,),
        in_specs=[spec(0), spec(1), spec(2), table, table] + [pl.BlockSpec(memory_space=pl.ANY)] * len(others),
        out_specs=[
            spec(0),
            pl.BlockSpec((1, 1, length), lambda h: (h, 0, 0)),
            pl.BlockSpec((3, 1, HD, length), lambda h: (0, h, 0, 0)),
        ],
        out_shape=[
            jax.ShapeDtypeStruct((heads * HD, length), bf16),
            jax.ShapeDtypeStruct((heads, 1, length), f32),
            jax.ShapeDtypeStruct((3, heads, HD, length), bf16),
        ],
        scratch_shapes=[pltpu.VMEM((length, HD), bf16)],
        compiler_params=pltpu.CompilerParams(vmem_limit_bytes=48 << 20),
        cost_estimate=pl.CostEstimate(flops=int(1.15e9 * (17)), bytes_accessed=1, transcendentals=0),
        name="attend_forward",
    )(projected, projected, projected, cosine, sine, *others)


def backward_kernel(block, qkv_ref, o_ref, g_ref, lse_ref, cos_ref, sin_ref, *refs):
    d_ref, sum_ref, kn_ref, vn_ref, dk_acc, dv_acc = refs
    blocks = o_ref.shape[1] // block
    kn_ref[...] = qkv_ref[1, 0].T
    vn_ref[...] = qkv_ref[2, 0].T

    def turn_back(values, cols):
        values = values.astype(bf16).astype(f32)
        return rotate(values, cos_ref[:, cols], -sin_ref[:, cols]).astype(bf16)

    for i in range(blocks):
        rows = pl.ds(i * block, block)
        q = qkv_ref[0, 0, :, rows] * jnp.asarray(HD**-0.5, bf16)
        g = g_ref[:, rows]
        lse = lse_ref[0, :, rows]
        delta = jnp.sum(g.astype(f32) * o_ref[:, rows].astype(f32), 0, keepdims=True)
        dq = None
        for j in range(i, -1, -1):
            cols = pl.ds(j * block, block)
            s = dot(kn_ref[cols, :], q, 1, 0)
            if j == i:
                s = causal(s)
            p = jnp.exp(s - lse)
            dp = dot(vn_ref[cols, :], g, 1, 0)
            ds = (p * (dp - delta)).astype(bf16)
            dv = dot(g, p.astype(bf16), 1, 1)
            dk = dot(q, ds, 1, 1)
            if j == i:
                dv_acc[:, cols] = dv
                dk_acc[:, cols] = dk
            else:
                dv_acc[:, cols] += dv
                dk_acc[:, cols] += dk
            part = dot(qkv_ref[1, 0, :, cols], ds, 1, 0)
            dq = part if dq is None else dq + part
        d_ref[0, 0, :, rows] = turn_back(dq * (HD**-0.5), rows)
    d_ref[1, 0] = turn_back(dk_acc[...], pl.ds(0, o_ref.shape[1]))
    d_ref[2, 0] = dv_acc[...].astype(bf16)
    for part in range(3):
        total = jnp.sum(d_ref[part, 0].astype(f32), 1, keepdims=True)
        sum_ref[part, 0] = jnp.broadcast_to(total, sum_ref.shape[2:])


def attend_backward(qkv, attn, d_attn, lse, cosine, sine, heads):
    length = qkv.shape[-1]
    block = length // 4
    one = pl.BlockSpec((HD, length), lambda h: (h, 0))
    three = pl.BlockSpec((3, 1, HD, length), lambda h: (0, h, 0, 0))
    table = pl.BlockSpec((ROT // 2, length), lambda h: (0, 0))
    return pl.pallas_call(
        functools.partial(backward_kernel, block),
        grid=(heads,),
        in_specs=[three, one, one, pl.BlockSpec((1, 1, length), lambda h: (h, 0, 0)), table, table],
        out_specs=[three, pl.BlockSpec((3, 1, HD, 128), lambda h: (0, h, 0, 0))],
        out_shape=[
            jax.ShapeDtypeStruct((3, heads, HD, length), bf16),
            jax.ShapeDtypeStruct((3, heads, HD, 128), f32),
        ],
        scratch_shapes=[pltpu.VMEM((length, HD), bf16)] * 2 + [pltpu.VMEM((HD, length), f32)] * 2,
        compiler_params=pltpu.CompilerParams(vmem_limit_bytes=48 << 20),
        cost_estimate=pl.CostEstimate(flops=int(1.15e9 * (28)), bytes_accessed=1, transcendentals=0),
        name="attend_backward",
    )(qkv, attn, d_attn, lse, cosine, sine)


def back_kernel(turned, core_ref, a_ref, wa_ref, b_ref, wb_ref, *refs):
    send_ref, keep_ref = refs[turned : turned + 2]
    side = 1 if turned else 0
    value = dot(a_ref[...], wa_ref[...], 0, side) + dot(b_ref[...], wb_ref[...], 0, side)
    if turned:
        hat_ref, sums_ref = refs[0], refs[3]

        @pl.when(pl.program_id(0) == 0)
        def _():
            sums_ref[...] = jnp.zeros_like(sums_ref)

        sums_ref[0:1] += jnp.sum(value * hat_ref[...].astype(f32), 0, keepdims=True)
        sums_ref[1:2] += jnp.sum(value, 0, keepdims=True)
    value = value.astype(bf16)
    rows = send_ref.shape[1]
    for core in range(2):

        @pl.when(core_ref[0] == core)
        def _():
            keep_ref[0] = value[core * rows : (core + 1) * rows]
            send_ref[0] = value[(1 - core) * rows : (2 - core) * rows]


def back_product(a, wa, b, wb, groups, hat=None):
    turned = hat is not None
    length, width = a.shape[1], wb.shape[0 if turned else 1]
    places = groups // 2
    block = length // places

    def left(value):
        return pl.BlockSpec((value.shape[0], block), lambda i, core: (0, i))

    def right(value):
        depth = value.shape[0]
        return pl.BlockSpec((width, depth) if turned else (depth, width), lambda i, core: (0, 0))

    half = jax.ShapeDtypeStruct((places, block // 2, width), bf16)
    core = (lax.axis_index("seq") % 2).astype(jnp.int32).reshape(1)
    hats = [hat] if turned else []
    return pl.pallas_call(
        functools.partial(back_kernel, turned),
        grid_spec=pltpu.PrefetchScalarGridSpec(
            num_scalar_prefetch=1,
            grid=(places,),
            in_specs=[left(a), right(a), left(b), right(b)]
            + [pl.BlockSpec((block, width), lambda i, core: (i, 0))] * len(hats),
            out_specs=[pl.BlockSpec((1, block // 2, width), lambda i, core: (i, 0, 0))] * 2
            + [pl.BlockSpec((8, width), lambda i, core: (0, 0))] * len(hats),
        ),
        out_shape=[half, half] + [jax.ShapeDtypeStruct((8, width), f32)] * len(hats),
        compiler_params=pltpu.CompilerParams(vmem_limit_bytes=56 << 20),
        cost_estimate=pl.CostEstimate(flops=int(1.15e9 * (27 if hats else 17)), bytes_accessed=1, transcendentals=0),
        name="back_product",
    )(core, a, wa, b, wb, *hats)


def normalise(values):
    average = jnp.mean(values, -1, keepdims=True)
    centred = values - average
    variance = jnp.mean(centred * centred, -1, keepdims=True)
    inverse = lax.rsqrt(variance + EPSILON)
    return centred * inverse, inverse


def gelu_tanh(values):
    scale, cubic = 0.7978845608028654, 0.044715
    curve = jnp.tanh(scale * (values + cubic * values * values * values))
    slope = 0.5 * (1.0 + curve) + 0.5 * values * (1.0 - curve * curve) * scale * (1.0 + 3.0 * cubic * values * values)
    return 0.5 * values * (1.0 + curve), slope


def rotate(parts, cosine, sine):
    half = ROT // 2
    first, second = parts[..., :half, :], parts[..., half:ROT, :]
    return jnp.concatenate(
        [first * cosine - second * sine, second * cosine + first * sine, parts[..., ROT:, :]], -2
    )


def swap(value, axes, size, bit):
    return lax.ppermute(value, axes, [(i, i ^ bit) for i in range(size)])


def gather_small(values, axis):
    index, count = lax.axis_index(axis), lax.axis_size(axis)
    block, bit = values[None], 1
    while bit < count:
        other = swap(block, axis, count, bit)
        high = (index & bit) > 0
        block = jnp.concatenate([jnp.where(high, other, block), jnp.where(high, block, other)], 0)
        bit *= 2
    return block


def scatter_small(values, size):
    index = lax.axis_index(BOTH)
    block = values
    bit = size // 2
    while bit:
        high = (index & bit) > 0
        low_half, high_half = block[:bit], block[bit:]
        other = swap(jnp.where(high, low_half, high_half), BOTH, size, bit)
        block = jnp.where(high, high_half, low_half) + other
        bit //= 2
    return block[0]


def gate(value, *others):
    anywhere = pl.BlockSpec(memory_space=pl.ANY)
    return pl.pallas_call(
        lambda *refs: None,
        in_specs=[anywhere] * (1 + len(others)),
        out_specs=anywhere,
        out_shape=jax.ShapeDtypeStruct(value.shape, value.dtype),
        input_output_aliases={0: 0},
        name="gate",
    )(value, *others)


def gather_pieces(own, wait=None):
    core = lax.axis_index("seq") % 2
    by_x = swap(own, "seq", 8, 2)
    by_y = swap(own, "seq", 8, 4)
    if wait:
        by_x = gate(by_x, *wait)
    relay = jnp.where(core == 0, by_y, by_x)
    diagonal = lax.ppermute(relay, "seq", [(i, i ^ (4 if i % 2 else 2)) for i in range(8)])
    mine = [own, by_x, by_y, diagonal]
    return [piece for one in mine for piece in (one, swap(one, "seq", 8, 1))]


def pieces_kernel(normed, order_ref, *refs):
    pieces = refs[:8]
    held = refs[-1]
    at = pl.program_id(0)
    for which, piece in enumerate(pieces):

        @pl.when(at == which)
        def _():
            held[...] = piece[...]

    if normed:
        gain_ref, shift_ref = refs[8:10]
        o_ref, hat_ref = refs[10:12]
        for at in range(0, held.shape[0], 32):
            rows = pl.ds(at, 32)
            value = normalise(held[rows, :].astype(f32))[0]
            hat_ref[rows, :] = value.astype(bf16)
            o_ref[rows, :] = (value * gain_ref[...] + shift_ref[...]).astype(bf16)


def put_in_order(pieces, *vectors, after=None):
    index = lax.axis_index("seq")
    order = jnp.stack([index ^ (2 * (which // 2)) ^ (which % 2) for which in range(8)]).astype(jnp.int32)
    rows, width = pieces[0].shape
    vectors = [vector.reshape(1, width) for vector in vectors]
    after = [] if after is None else [after]
    outs = 2 if vectors else 1
    return pl.pallas_call(
        functools.partial(pieces_kernel, bool(vectors)),
        grid_spec=pltpu.PrefetchScalarGridSpec(
            num_scalar_prefetch=1,
            grid=(8,),
            in_specs=[pl.BlockSpec((rows, width), lambda i, order: (0, 0))] * 8
            + [pl.BlockSpec((1, width), lambda i, order: (0, 0))] * len(vectors)
            + [pl.BlockSpec(memory_space=pl.ANY)] * len(after),
            out_specs=[pl.BlockSpec((rows, width), lambda i, order: (order[i], 0))] * outs,
            scratch_shapes=[pltpu.VMEM((rows, width), bf16)] * (len(vectors) > 0),
        ),
        out_shape=[jax.ShapeDtypeStruct((8 * rows, width), bf16)] * outs,
        compiler_params=pltpu.CompilerParams(vmem_limit_bytes=40 << 20),
        cost_estimate=pl.CostEstimate(flops=int(1.15e9 * (10)), bytes_accessed=1, transcendentals=0),
        name="put_in_order",
    )(order, *pieces, *vectors, *after)


def take(values, index, axis):
    return lax.dynamic_index_in_dim(values, index, axis, keepdims=False)


def sum_core(send, keep):
    return keep.astype(f32) + swap(send, "seq", 8, 1).astype(f32)


def sum_sends(cells):
    index = lax.axis_index("seq")
    x, y = (index // 2) % 2, index // 4
    half = cells.shape[2] // 2
    cells = cells.reshape(2, 2, *cells.shape[1:])
    left, right = cells[..., :half], cells[..., half:]
    sends = take(left, 1 - x, 1).astype(bf16), take(right, 1 - y, 0).astype(bf16)
    return sends, (take(left, x, 1), take(right, y, 0))


def sum_start(sends, stays):
    got_left, got_right = swap(sends[0], "seq", 8, 2), swap(sends[1], "seq", 8, 4)
    return stays[0] + got_left.astype(f32), stays[1] + got_right.astype(f32)


def sum_end(left, right):
    index = lax.axis_index("seq")
    x, y = (index // 2) % 2, index // 4
    got_left = swap(take(left, 1 - y, 0).astype(bf16), "seq", 8, 4)
    got_right = swap(take(right, 1 - x, 0).astype(bf16), "seq", 8, 2)
    left = take(left, y, 0) + got_left.astype(f32)
    right = take(right, x, 0) + got_right.astype(f32)
    return jnp.concatenate([left, right], -1)


def spread_kernel(blocks, groups, width, w_ref, o_ref):
    step = max(1, 128 // width)
    for group in range(groups):
        for at in range(0, blocks, step):
            parts = [w_ref[:, pl.ds(((at + k) * groups + group) * width, width)] for k in range(step)]
            o_ref[group, :, pl.ds(at * width, step * width)] = parts[0] if step == 1 else jnp.concatenate(parts, 1)


def collect_kernel(blocks, groups, width, g_ref, o_ref):
    step = max(1, 128 // width)
    for at in range(blocks):
        for group in range(0, groups, step):
            parts = [g_ref[group + k, :, pl.ds(at * width, width)].astype(f32) for k in range(step)]
            where = pl.ds((at * groups + group) * width, step * width)
            o_ref[:, where] = parts[0] if step == 1 else jnp.concatenate(parts, 1)


def local_call(kernel, shape, dtype, *args):
    return pl.pallas_call(
        kernel,
        out_shape=jax.ShapeDtypeStruct(shape, dtype),
        compiler_params=pltpu.CompilerParams(vmem_limit_bytes=32 << 20),
        name="regroup",
    )(*args)


def by_group(weight, blocks, groups):
    rows, width = weight.shape[0], weight.shape[1] // (blocks * groups)
    kernel = functools.partial(spread_kernel, blocks, groups, width)
    out = local_call(kernel, (groups, rows, blocks * width), bf16, weight)
    return out.reshape(groups * rows, blocks * width)


def trade(values):
    return lax.all_to_all(values, "seq", split_axis=0, concat_axis=0, tiled=True)


def to_rows(grads, groups, blocks):
    rows, width = grads.shape[0] // groups, grads.shape[1] // blocks
    got = grads.reshape(groups, rows, blocks * width)
    kernel = functools.partial(collect_kernel, blocks, groups, width)
    return local_call(kernel, (rows, blocks * groups * width), f32, got)


def local(
    block_input,
    ln_gain,
    norm_layer_bias,
    query_key_value_weight,
    query_key_value_bias,
    attention_output_weight,
    attention_output_bias,
    first_feed_weight,
    first_feed_bias,
    second_feed_weight,
    second_feed_bias,
    cotangent,
):
    shards, groups = lax.axis_size("fsdp"), lax.axis_size("seq")
    size = shards * groups
    me = lax.axis_index("seq")
    _, piece, width = block_input.shape
    length = piece * groups
    heads = H // groups
    rows = query_key_value_weight.shape[0]
    hidden_rows = second_feed_weight.shape[0]
    hidden = shards * hidden_rows
    out_rows = attention_output_weight.shape[0]
    whole_heads = out_rows == HD and heads == shards

    x_own, g_own = block_input[0], cotangent[0]
    vectors = (
        ln_gain,
        norm_layer_bias,
        query_key_value_bias,
        attention_output_bias,
        first_feed_bias,
        second_feed_bias,
    )
    small = gather_small(jnp.concatenate(vectors), "fsdp")
    small = gather_small(small, "seq").astype(f32)
    pieces, at = [], 0
    for vector in vectors:
        part = small[:, :, at : at + vector.shape[0]]
        pieces.append(part.transpose(1, 0, 2).reshape(-1))
        at += vector.shape[0]
    gain, shift, bqkv, bout, bfc1, bfc2 = pieces
    bqkv = take(bqkv.reshape(3, heads, groups, HD), me, 2).reshape(-1)
    bfc1 = take(bfc1.reshape(shards, groups, hidden_rows), me, 1).reshape(-1)
    inner = 3 * heads * HD
    wfc2 = lax.all_gather(second_feed_weight, "fsdp", axis=0, tiled=True)
    wfc1 = trade(by_group(first_feed_weight, shards, groups))
    wfc1 = lax.all_gather(gate(wfc1, wfc2), "fsdp", axis=0, tiled=True)
    first = trade(by_group(query_key_value_weight, 3 * heads, groups))
    if whole_heads:
        first = jnp.concatenate([first, attention_output_weight.reshape(groups * rows, -1)], 1)
    first = lax.all_gather(gate(first, wfc1), "fsdp", axis=0, tiled=True)
    if groups == 8:
        x_pieces = gather_pieces(x_own)
        normed_all, hat_all = put_in_order(x_pieces, gain, shift)
        (g_all,) = put_in_order(gather_pieces(gate(g_own, normed_all)))
    else:
        x_all = lax.all_gather(x_own, "seq", axis=0, tiled=True)
        hat_all = normalise(x_all.astype(f32))[0]
        normed_all = (hat_all * gain + shift).astype(bf16)
        g_all = lax.all_gather(g_own, "seq", axis=0, tiled=True)

    up_pre = dot(wfc1, normed_all, 0, 1) + bfc1[:, None]
    up, slope = gelu_tanh(up_pre)
    up = up.astype(bf16)
    term_wfc2 = dot(up, g_all, 1, 0).astype(bf16)
    d_pre = (dot(wfc2, g_all, 1, 1) * slope).astype(bf16)
    term_wfc1 = dot(normed_all, d_pre, 0, 1).astype(bf16)
    folds = width // hidden
    term_wfc1 = jnp.split(term_wfc1.reshape(shards, -1, hidden), folds, 1)
    both = jnp.concatenate([term_wfc2.reshape(shards, -1, width), jnp.concatenate(term_wfc1, 2)], 1)
    both = lax.psum_scatter(both.reshape(-1, width), "fsdp", scatter_dimension=0, tiled=True)
    grad_wfc2 = both[:hidden_rows]
    grad_wfc1 = jnp.concatenate(jnp.split(both[hidden_rows:], folds, 1), 0)

    weights_a = first
    wqkv = first[:, :inner]
    if whole_heads:
        wout = first[:, inner:].reshape(heads * HD, width)
    else:
        wout = lax.all_gather(attention_output_weight, BOTH, axis=0, tiled=True)
        wout = take(wout.reshape(heads, groups, HD, width), me, 1).reshape(heads * HD, width)
    freqs = 10000.0 ** (-2.0 * jnp.arange(ROT // 2).astype(f32) / ROT)
    angles = freqs[:, None] * jnp.arange(length).astype(f32)[None, :]
    cosine, sine = jnp.cos(angles), jnp.sin(angles)
    projected = dot(wqkv, normed_all, 0, 1) + bqkv[:, None]
    attn, lse, qkv = attend_forward(projected, cosine, sine, heads)
    d_attn = dot(wout, g_all, 1, 1).astype(bf16)
    d_proj, sum_proj = attend_backward(qkv, attn, d_attn, lse, cosine, sine, heads)
    d_proj, sum_proj = d_proj.reshape(inner, length), sum_proj[..., 0].reshape(inner)
    term_a = dot(normed_all, d_proj, 0, 1).astype(bf16)
    term_wout = dot(attn, g_all, 1, 0).astype(bf16)
    if whole_heads:
        term_a = jnp.concatenate([term_a, term_wout.reshape(width, -1)], 1)
    else:
        mask = (jnp.arange(groups) == me).astype(bf16)
        spread = term_wout.reshape(heads, 1, HD, width) * mask[None, :, None, None]
        spread = spread.reshape(H * HD, width)
        grad_wout = lax.psum_scatter(spread, BOTH, scatter_dimension=0, tiled=True).astype(f32)
    first = lax.psum_scatter(gate(term_a, both), "fsdp", scatter_dimension=0, tiled=True)

    if groups == 8:
        mixed = back_product(attn, wout, up, wfc2, groups)
        *d_normed, sums = back_product(d_proj, weights_a, d_pre, wfc1, groups, hat_all)
        mixed = sum_end(*sum_start(*sum_sends(sum_core(*mixed))))
        d_normed = sum_end(*sum_start(*sum_sends(sum_core(*d_normed))))
    else:
        mixed = dot(attn, wout, 0, 0) + dot(up, wfc2, 0, 0)
        d_normed = dot(d_proj, wqkv, 0, 1) + dot(d_pre, wfc1, 0, 1)
        sums = jnp.stack([jnp.sum(d_normed * hat_all, 0), jnp.sum(d_normed, 0)])
        d_normed, mixed = (
            lax.psum_scatter(v.astype(bf16), "seq", scatter_dimension=0, tiled=True).astype(f32)
            for v in (d_normed, mixed)
        )
    traded = trade(grad_wfc1)
    rows_wfc1 = to_rows(traded, groups, shards)
    grad_wfc2 = grad_wfc2.astype(f32)

    here = (jnp.arange(groups) == me).astype(f32)
    term_bqkv = sum_proj.reshape(3 * heads, 1, HD) * here[None, :, None]
    term_bqkv = term_bqkv.reshape(-1)
    term_bfc1 = (jnp.sum(d_pre.astype(f32), 1).reshape(shards, 1, hidden_rows) * here[None, :, None]).reshape(-1)
    terms = (
        sums[0],
        sums[1],
        term_bqkv[: 2 * H * HD],
        term_bqkv[2 * H * HD :],
        jnp.sum(g_own.astype(f32), 0),
        term_bfc1,
    )
    summed = jnp.concatenate([t.reshape(size, -1) for t in terms], 1)
    summed = scatter_small(summed, size)
    vector_grads, at = [], 0
    for term in terms:
        count = term.shape[0] // size
        vector_grads.append(summed[at : at + count])
        at += count
    grad_gain, grad_shift, grad_bqk, grad_bv, grad_bout, grad_bfc1 = vector_grads

    first = gate(first, d_normed, mixed, traded, summed)
    if whole_heads:
        grad_wout = first[:, inner:].reshape(out_rows, width).astype(f32)
    grad_wqkv = to_rows(trade(first[:, :inner]), groups, 3 * heads)
    block_output = (x_own.astype(f32) + mixed + bout + bfc2).astype(bf16)
    xhat, inverse = normalise(x_own.astype(f32))
    e = d_normed * gain
    d_x = (e - jnp.mean(e, -1, keepdims=True) - xhat * jnp.mean(e * xhat, -1, keepdims=True)) * inverse
    grad_input = g_own.astype(f32) + d_x
    return (
        block_output[None],
        grad_input[None],
        grad_gain,
        grad_shift,
        grad_wqkv,
        grad_bqk,
        grad_bv,
        grad_wout,
        grad_bout,
        rows_wfc1,
        grad_bfc1,
        grad_wfc2,
        grad_bout,
    )


def solution(mesh):
    tokens, split = P("fsdp", "seq", None), P(BOTH)
    return jax.shard_map(
        local,
        mesh=mesh,
        in_specs=(tokens, *([split] * 10), tokens),
        out_specs=(tokens, tokens, *([split] * 11)),
        check_vma=False,
    )
```

time: 557 us -> 541 us (0.971)
  waiting for transfers between devices: 92.4 us -> 192 us
  local copies, waits for them, and re-layouts: 114 us -> 28.5 us
  Pallas kernels: 43.3 us -> 115 us
  matrix products: 149 us -> 88.2 us
  blocking collectives: 37.2 us -> 0 us
  other arithmetic: 64.6 us -> 47.4 us
  starting transfers between devices: 35.6 us -> 49.4 us
    pallas_call x0 -> x13, Pallas kernels: none -> 69.5 us  [the longest x2 43.6 us: back_product(): pl.pallas_call(functools.partial(back_kernel, turned), grid_spec=pltpu.Pr...]
    dot_general x12 -> x8, matrix products: 149 us -> 88.2 us  [dot(): lax.dot_general(a, b, (((ca,), (cb,)), ((), ())), preferred_element_type=...]
    ppermute x26 -> x32, waiting for transfers between devices: 74.2 us -> 112 us  [swap(): return lax.ppermute(value, axes, [(i, i ^ bit) for i in range(size)])]
    all_to_all x2 -> x0, blocking collectives: 37.2 us -> none  [to_columns(): return lax.all_to_all(sent, 'seq', split_axis=0, concat_axis=0, tiled=True)]
    dynamic_update_slice x12 -> x0, local copies, waits for them, and re-layouts: 27.4 us -> none  [the longest x8 12.4 us: gather_tokens(): mine = lax.dynamic_update_index_in_dim(mine, piece, place ^ shift, 0)]
    all_gather x1, waiting for transfers between devices: 0.01 us -> 24.4 us  [local(): wfc2 = lax.all_gather(second_feed_weight, 'fsdp', axis=0, tiled=True)]
    all_gather x3 -> x2, waiting for transfers between devices: 0.01 us -> 21.5 us  [the longest x1 18.8 us: local(): first = lax.all_gather(gate(first, wfc1), 'fsdp', axis=0, tiled=True)]
    convert_element_type x13 -> x9, local copies, waits for them, and re-layouts: 22.6 us -> 2.79 us  [the longest x2 1.29 us: sum_sends(): take(right, 1 - y, 0).astype(bf16)]
  transfers between devices with their start and end apart: 38 -> 43, of which waited for: 11 -> 21; matrix products, arithmetic and copies ran while one was open for 55% -> 28% of each run, Pallas kernels for 8% -> 21%
where the time goes in v2:
time: 541 us; the launch traced here: 535 us
  waiting for transfers between devices  192 us (35%)
  Pallas kernels  115 us (21%)
  matrix products  88.2 us (16%)
  starting transfers between devices  49.4 us (9%)
  other arithmetic  47.4 us (9%)
  local copies, waits for them, and re-layouts  28.5 us (5%)
  between operations  15.2 us (3%)
    ppermute x32, waiting for transfers between devices, swap(): return lax.ppermute(value, axes, [(i, i ^ bit) for i in range(size)])  112 us
    dot_general x8, matrix products, dot(): lax.dot_general(a, b, (((ca,), (cb,)), ((), ())), preferred_element_type=...  88.2 us
    pallas_call x2, Pallas kernels, back_product(): pl.pallas_call(functools.partial(back_kernel, turned), grid_spec=pltpu.Pr...  43.6 us
    ppermute x32, starting transfers between devices, swap(): return lax.ppermute(value, axes, [(i, i ^ bit) for i in range(size)])  33.2 us
    pallas_call x1, Pallas kernels, attend_backward(): pl.pallas_call(functools.partial(backward_kernel, block), grid=(heads,),...  28 us
    all_gather x1, waiting for transfers between devices, local(): wfc2 = lax.all_gather(second_feed_weight, 'fsdp', axis=0, tiled=True)  24.4 us
    pallas_call x2, Pallas kernels, put_in_order(): pl.pallas_call(functools.partial(pieces_kernel, bool(vectors)), grid_spec...  20.8 us
    all_to_all x4, waiting for transfers between devices, trade(): lax.all_to_all(values, 'seq', split_axis=0, concat_axis=0, tiled=True)  19 us
  transfers between devices with their start and end apart: 43, of which 21 were waited for; matrix products, arithmetic and copies ran while one was open for 28% of the time, Pallas kernels for 21%

profile of v2, /device:TPU:0, one launch (start us, length us, event | category | flops | bytes accessed | tf_op | source)
XLA Modules:
  0.0 535.2 jit_solution(2327666751387875519)
XLA Ops:
  12.5 21.9 %collective-permute-done.1.refs_2_ = bf16[256,2048]{1,0:T(8,128)(2,1)S(1)} collective-permute-done((bf16[256,2048]{1,0:T(8,128)(2,1)}, bf16[256,2048]{1,0:T(8,128)(2,1)S(1)}, u32[]{:S(2)}, u32[]{:S(2)}) %collective-permute-start.1) | collective-permute-done | bytes 1048608 | tf_op jit(solution)/shard_map/ppermute | solution.py:238
  54.3 10.6 %collective-permute-done.10 = bf16[2,4,704]{2,1,0:T(4,128)(2,1)S(1)} collective-permute-done((bf16[2,4,704]{2,1,0:T(4,128)(2,1)S(1)}, bf16[2,4,704]{2,1,0:T(4,128)(2,1)S(1)}, u32[]{:S(2)}, u32[]{:S(2)}) %collective-permute-start.10) | collective-permute-done | bytes 11296 | tf_op jit(solution)/shard_map/ppermute | solution.py:238
  68.9 24.4 %all-gather.4.cloned.1.call-done.refs_1_.wb_ref = bf16[1024,2048]{1,0:T(8,128)(2,1)} async-done(((bf16[256,2048]{1,0:T(8,128)(2,1)}), bf16[1024,2048]{1,0:T(8,128)(2,1)}) %all-gather.4.cloned.1.call-update) | async-done | bytes 4194320 | tf_op jit(solution)/shard_map/all_gather | solution.py:457
  94.8 13.0 %put_in_order.2 = (bf16[2048,2048]{1,0:T(8,128)(2,1)}, bf16[2048,2048]{1,0:T(8,128)(2,1)}) custom-call(s32[8]{0:T(128)S(1)} %stack.44.order_ref, bf16[256,2048]{1,0:T(8,128)(2,1)S(1)} %bitcast.128, bf16[256,2048]{1,0:T(8,128)(2,1)} %collective-permute-done.refs_1_, bf16[256,2048]{1,0:T(8,128)(2,1)S(1)} %collective-permute-done.1.refs_2_, ...), custom_call_target="tpu_custom_call" | custom-call | flops 11500000256 | bytes 1 | tf_op jit(solution)/shard_map/put_in_order/pallas_call | solution.py:316
  110.9 22.1 %collective-permute-done.18.refs_2_ = bf16[256,2048]{1,0:T(8,128)(2,1)S(1)} collective-permute-done((bf16[256,2048]{1,0:T(8,128)(2,1)}, bf16[256,2048]{1,0:T(8,128)(2,1)S(1)}, u32[]{:S(2)}, u32[]{:S(2)}) %collective-permute-start.18) | collective-permute-done | bytes 1048608 | tf_op jit(solution)/shard_map/ppermute | solution.py:238
  146.9 8.7 %collective-permute-done.22.refs_6_ = bf16[256,2048]{1,0:T(8,128)(2,1)} collective-permute-done((bf16[256,2048]{1,0:T(8,128)(2,1)}, bf16[256,2048]{1,0:T(8,128)(2,1)}, u32[]{:S(2)}, u32[]{:S(2)}) %collective-permute-start.22) | collective-permute-done | bytes 1048608 | tf_op jit(solution)/shard_map/ppermute | solution.py:284
  164.3 7.7 %put_in_order.3 = bf16[2048,2048]{1,0:T(8,128)(2,1)} custom-call(s32[8]{0:T(128)S(1)} %stack.44.order_ref, bf16[256,2048]{1,0:T(8,128)(2,1)S(1)} %copy-done.4, bf16[256,2048]{1,0:T(8,128)(2,1)} %collective-permute-done.17.refs_1_, bf16[256,2048]{1,0:T(8,128)(2,1)S(1)} %collective-permute-done.18.refs_2_, bf16[256,2048]{1,0:T(8,128)(2,1)} %collective-permute-done.19.refs_3_, ...), custom_call_target="tpu_custom_call" | custom-call | flops 11500000256 | bytes 1 | tf_op jit(solution)/shard_map/put_in_order/pallas_call | solution.py:316
  175.0 16.7 %multiply_convert_fusion = (bf16[1024,2048]{1,0:T(8,128)(2,1)}, f32[1024,2048]{1,0:T(8,128)S(1)}) fusion(f32[1024]{0:T(1024)S(1)} %bitcast.144, bf16[2048,1024]{1,0:T(8,128)(2,1)} %all-gather.6.cloned.1.call-done.refs_1_.wb_ref, bf16[2048,2048]{1,0:T(8,128)(2,1)} %get-tuple-element.25.refs_1_), kind=kOutput, calls=%fused_computation.13 | convolution fusion | flops 8610906112 | bytes 25169920 | tf_op jit(solution)/shard_map/dot_general | solution.py:20
  191.7 15.2 %convert_reduce_fusion = (f32[1024]{0:T(1024)S(1)}, bf16[1024,2048]{1,0:T(8,128)(2,1)}) fusion(f32[1024,2048]{1,0:T(8,128)S(1)} %get-tuple-element.75, f32[1024]{0:T(1024)S(1)} %bitcast.145, bf16[2048,2048]{1,0:T(8,128)(2,1)} %put_in_order.3, bf16[1024,2048]{1,0:T(8,128)(2,1)S(1)} %copy-done.25), kind=kOutput, calls=%fused_computation.10 | convolution fusion | flops 8636070912 | bytes 25174016 | tf_op jit(solution)/shard_map/dot_general | solution.py:20
  207.6 12.8 %convolution_convert_fusion.1 = bf16[2048,1024]{1,0:T(8,128)(2,1)S(1)} fusion(bf16[2048,2048]{1,0:T(8,128)(2,1)} %get-tuple-element.25.refs_1_, bf16[1024,2048]{1,0:T(8,128)(2,1)} %get-tuple-element.77.b_ref), kind=kOutput, calls=%fused_computation.16 | convolution fusion | flops 8592031744 | bytes 16777216 | tf_op jit(solution)/shard_map/dot_general | solution.py:20
  222.6 11.2 %convolution_convert_fusion = bf16[1024,2048]{1,0:T(8,128)(2,1)S(1)} fusion(bf16[1024,2048]{1,0:T(8,128)(2,1)S(1)} %copy-done.47, bf16[2048,2048]{1,0:T(8,128)(2,1)} %put_in_order.3), kind=kOutput, calls=%fused_computation.15 | convolution fusion | flops 8592031744 | bytes 16777216 | tf_op jit(solution)/shard_map/dot_general | solution.py:20
  237.5 18.8 %all-gather.8.cloned.1.call-done.wa_ref = bf16[2048,1024]{1,0:T(8,128)(2,1)} async-done(((bf16[512,1024]{1,0:T(8,128)(2,1)}), bf16[2048,1024]{1,0:T(8,128)(2,1)}) %all-gather.8.cloned.1.call-update) | async-done | bytes 4194320 | tf_op jit(solution)/shard_map/all_gather | solution.py:463
  256.2 12.5 %convolution_add_fusion.q_ref.k_ref.v_ref = f32[768,2048]{1,0:T(8,128)} fusion(bf16[2048,2048]{1,0:T(8,128)(2,1)} %get-tuple-element.25.refs_1_, bf16[2048,1024]{1,0:T(8,128)(2,1)} %all-gather.8.cloned.1.call-done.wa_ref, f32[768]{0:T(1024)S(1)} %add.178), kind=kOutput, calls=%fused_computation.17 | convolution fusion | flops 6444023808 | bytes 17828864 | tf_op jit(solution)/shard_map/dot_general | solution.py:20
  275.4 17.1 %attend_forward.1 = (bf16[256,2048]{1,0:T(8,128)(2,1)S(1)}, f32[4,1,2048]{2,1,0:T(1,128)S(1)}, bf16[3,4,64,2048]{3,2,1,0:T(8,128)(2,1)S(1)}) custom-call(f32[768,2048]{1,0:T(8,128)} %convolution_add_fusion.q_ref.k_ref.v_ref, f32[768,2048]{1,0:T(8,128)} %convolution_add_fusion.q_ref.k_ref.v_ref, f32[768,2048]{1,0:T(8,128)} %convolution_add_fusion.q_ref.k_ref.v_ref, ...), custom_call_target="tpu_custom_call" | custom-call | flops 19549999104 | bytes 1 | tf_op jit(solution)/shard_map/attend_forward/pallas_call | solution.py:72
  294.3 28.0 %attend_backward.1 = (bf16[3,4,64,2048]{3,2,1,0:T(8,128)(2,1)S(1)}, f32[3,4,64,128]{3,2,1,0:T(8,128)S(1)}) custom-call(bf16[3,4,64,2048]{3,2,1,0:T(8,128)(2,1)} %copy-done.13, bf16[256,2048]{1,0:T(8,128)(2,1)S(1)} %get-tuple-element.26.a_ref.o_ref, bf16[256,2048]{1,0:T(8,128)(2,1)S(1)} %convolution_convert_fusion.4.g_ref, ...), custom_call_target="tpu_custom_call" | custom-call | flops 32199999488 | bytes 1 | tf_op jit(solution)/shard_map/attend_backward/pallas_call | solution.py:142
  324.0 26.5 %back_product.3 = (bf16[4,256,2048]{2,1,0:T(8,128)(2,1)}, bf16[4,256,2048]{2,1,0:T(8,128)(2,1)}, f32[8,2048]{1,0:T(8,128)}) custom-call(s32[1]{0:T(128)} %bitcast.core_ref, bf16[768,2048]{1,0:T(8,128)(2,1)} %bitcast.130, bf16[2048,1024]{1,0:T(8,128)(2,1)} %all-gather.8.cloned.1.call-done.wa_ref, bf16[1024,2048]{1,0:T(8,128)(2,1)} %get-tuple-element.77.b_ref, ...), custom_call_target="tpu_custom_call" | custom-call | flops 31050000384 | bytes 1 | tf_op jit(solution)/shard_map/back_product/pallas_call | solution.py:197
  358.3 17.1 %back_product.2 = (bf16[4,256,2048]{2,1,0:T(8,128)(2,1)}, bf16[4,256,2048]{2,1,0:T(8,128)(2,1)}) custom-call(s32[1]{0:T(128)} %bitcast.core_ref, bf16[256,2048]{1,0:T(8,128)(2,1)} %copy-done.11, bf16[256,2048]{1,0:T(8,128)(2,1)} %copy-done.27, bf16[1024,2048]{1,0:T(8,128)(2,1)} %get-tuple-element.74.b_ref, ...), custom_call_target="tpu_custom_call" | custom-call | flops 19549999104 | bytes 1 | tf_op jit(solution)/shard_map/back_product/pallas_call | solution.py:197
  377.2 11.2 %convolution_convert_fusion.2 = bf16[2048,768]{1,0:T(8,128)(2,1)} fusion(bf16[2048,2048]{1,0:T(8,128)(2,1)} %get-tuple-element.25.refs_1_, bf16[768,2048]{1,0:T(8,128)(2,1)S(1)} %bitcast.131), kind=kOutput, calls=%fused_computation.18 | convolution fusion | flops 6444023808 | bytes 14680064 | tf_op jit(solution)/shard_map/dot_general | solution.py:20
  424.7 13.3 %collective-permute-done.27 = bf16[2,256,1024]{2,1,0:T(8,128)(2,1)} collective-permute-done((bf16[2,256,1024]{2,1,0:T(8,128)(2,1)}, bf16[2,256,1024]{2,1,0:T(8,128)(2,1)}, u32[]{:S(2)}, u32[]{:S(2)}) %collective-permute-start.27) | collective-permute-done | bytes 1048608 | tf_op jit(solution)/shard_map/ppermute | solution.py:238
  444.4 16.0 %collective-permute-done.15 = bf16[2,256,1024]{2,1,0:T(8,128)(2,1)S(1)} collective-permute-done((bf16[2,256,1024]{2,1,0:T(8,128)(2,1)S(1)}, bf16[2,256,1024]{2,1,0:T(8,128)(2,1)S(1)}, u32[]{:S(2)}, u32[]{:S(2)}) %collective-permute-start.15) | collective-permute-done | bytes 1048608 | tf_op jit(solution)/shard_map/ppermute | solution.py:238
  464.5 8.6 %collective-permute-done.28 = bf16[256,1024]{1,0:T(8,128)(2,1)S(1)} collective-permute-done((bf16[256,1024]{1,0:T(8,128)(2,1)S(1)}, bf16[256,1024]{1,0:T(8,128)(2,1)S(1)}, u32[]{:S(2)}, u32[]{:S(2)}) %collective-permute-start.28) | collective-permute-done | bytes 524320 | tf_op jit(solution)/shard_map/ppermute | solution.py:238
  473.5 9.2 %collective-permute-done.16 = bf16[256,1024]{1,0:T(8,128)(2,1)S(1)} collective-permute-done((bf16[256,1024]{1,0:T(8,128)(2,1)S(1)}, bf16[256,1024]{1,0:T(8,128)(2,1)S(1)}, u32[]{:S(2)}, u32[]{:S(2)}) %collective-permute-start.16) | collective-permute-done | bytes 524320 | tf_op jit(solution)/shard_map/ppermute | solution.py:238
  497.9 9.1 %all-to-all-done.2.g_ref = bf16[8,64,1024]{2,1,0:T(8,128)(2,1)S(1)} async-done(((bf16[8,64,1024]{2,1,0:T(8,128)(2,1)}), bf16[8,64,1024]{2,1,0:T(8,128)(2,1)S(1)}, u32[]{:S(2)}, u32[]{:S(2)}) %all-to-all-start.2) | async-done | bytes 1048608 | tf_op jit(solution)/shard_map/all_to_all | solution.py:401
  519.9 6.4 %all-to-all-done.3.g_ref = bf16[8,64,768]{2,1,0:T(8,128)(2,1)S(1)} async-done(((bf16[8,64,768]{2,1,0:T(8,128)(2,1)}), bf16[8,64,768]{2,1,0:T(8,128)(2,1)S(1)}, u32[]{:S(2)}, u32[]{:S(2)}) %all-to-all-start.3) | async-done | bytes 786464 | tf_op jit(solution)/shard_map/all_to_all | solution.py:401
  (302 shorter events, 161.9 us)
Async XLA Ops:
  7.3 86.0 %all-gather.4.cloned.1.call-start = ((), (), s32[]{:S(2)}) async-start(), calls=%async_computation.6 | async-start | bytes 5242880 | tf_op jit(solution)/shard_map/all_gather | solution.py:457
  8.0 26.4 %collective-permute-start.1 = (bf16[256,2048]{1,0:T(8,128)(2,1)}, bf16[256,2048]{1,0:T(8,128)(2,1)S(1)}, u32[]{:S(2)}, u32[]{:S(2)}) collective-permute-start(bf16[256,2048]{1,0:T(8,128)(2,1)} %bitcast.125), channel_id=1, source_target_pairs={{0,2},{1,3},{2,0},{3,1},{4,6},{5,7},{6,4},{7,5},{8,10},{9,11},{10,... | collective-permute-start | bytes 3145736 | tf_op jit(solution)/shard_map/ppermute | solution.py:238
  11.0 24.9 %collective-permute-start.3 = (bf16[256,2048]{1,0:T(8,128)(2,1)}, bf16[256,2048]{1,0:T(8,128)(2,1)}, u32[]{:S(2)}, u32[]{:S(2)}) collective-permute-start(bf16[256,2048]{1,0:T(8,128)(2,1)} %bitcast.126), channel_id=1, source_target_pairs={{0,4},{1,5},{2,6},{3,7},{4,0},{5,1},{6,2},{7,3},{8,12},{9,13},{10,... | collective-permute-start | bytes 3145736 | tf_op jit(solution)/shard_map/ppermute | solution.py:238
  46.7 22.3 %all-to-all-start.1 = ((bf16[8,64,1024]{2,1,0:T(8,128)(2,1)}), bf16[8,64,1024]{2,1,0:T(8,128)(2,1)S(1)}, u32[]{:S(2)}, u32[]{:S(2)}) async-start(bf16[8,64,1024]{2,1,0:T(8,128)(2,1)} %regroup.5), calls=%async_computation.1 | async-start | bytes 2097152 | tf_op jit(solution)/shard_map/all_to_all | solution.py:401
  50.2 124.5 %all-gather.6.cloned.1.call-start = ((), (), s32[]{:S(2)}) async-start(), calls=%async_computation.7 | async-start | bytes 5242880 | tf_op jit(solution)/shard_map/all_gather | solution.py:459
  50.8 44.0 %collective-permute-start = (bf16[256,2048]{1,0:T(8,128)(2,1)S(1)}, bf16[256,2048]{1,0:T(8,128)(2,1)}, u32[]{:S(2)}, u32[]{:S(2)}) collective-permute-start(bf16[256,2048]{1,0:T(8,128)(2,1)S(1)} %bitcast.127), channel_id=1, source_target_pairs={{0,1},{1,0},{2,3},{3,2},{4,5},{5,4},{6,7},{7,6},{8,9},{9,8},{10,11... | collective-permute-start | bytes 3145736 | tf_op jit(solution)/shard_map/ppermute | solution.py:238
  51.6 43.2 %collective-permute-start.2 = (bf16[256,2048]{1,0:T(8,128)(2,1)S(1)}, bf16[256,2048]{1,0:T(8,128)(2,1)}, u32[]{:S(2)}, u32[]{:S(2)}) collective-permute-start(bf16[256,2048]{1,0:T(8,128)(2,1)S(1)} %collective-permute-done.1.refs_2_), channel_id=1, source_target_pairs={{0,1},{1,0},{2,3},{3,2},{4,5},{5,4},{6,7},{7,6},{8,9},{9,8},{10,11... | collective-permute-start | bytes 3145736 | tf_op jit(solution)/shard_map/ppermute | solution.py:238
  52.0 42.8 %collective-permute-start.4 = (bf16[256,2048]{1,0:T(8,128)(2,1)}, bf16[256,2048]{1,0:T(8,128)(2,1)}, u32[]{:S(2)}, u32[]{:S(2)}) collective-permute-start(bf16[256,2048]{1,0:T(8,128)(2,1)} %collective-permute-done.3.refs_4_), channel_id=1, source_target_pairs={{0,1},{1,0},{2,3},{3,2},{4,5},{5,4},{6,7},{7,6},{8,9},{9,8},{10,11... | collective-permute-start | bytes 3145736 | tf_op jit(solution)/shard_map/ppermute | solution.py:238
  53.4 41.5 %collective-permute-start.6 = (bf16[256,2048]{1,0:T(8,128)(2,1)}, bf16[256,2048]{1,0:T(8,128)(2,1)}, u32[]{:S(2)}, u32[]{:S(2)}) collective-permute-start(bf16[256,2048]{1,0:T(8,128)(2,1)} %collective-permute-done.5.refs_6_), channel_id=1, source_target_pairs={{0,1},{1,0},{2,3},{3,2},{4,5},{5,4},{6,7},{7,6},{8,9},{9,8},{10,11... | collective-permute-start | bytes 3145736 | tf_op jit(solution)/shard_map/ppermute | solution.py:238
  65.0 28.4 %collective-permute-start.11 = (bf16[4,4,704]{2,1,0:T(4,128)(2,1)S(1)}, bf16[4,4,704]{2,1,0:T(4,128)(2,1)S(1)}, u32[]{:S(2)}, u32[]{:S(2)}) collective-permute-start(bf16[4,4,704]{2,1,0:T(4,128)(2,1)S(1)} %pad_maximum_fusion.5), channel_id=1, source_target_pairs={{0,4},{1,5},{2,6},{3,7},{4,0},{5,1},{6,2},{7,3},{8,12},{9,13},{10,... | collective-permute-start | bytes 67592 | tf_op jit(solution)/shard_map/ppermute | solution.py:238
  107.9 25.1 %collective-permute-start.18 = (bf16[256,2048]{1,0:T(8,128)(2,1)}, bf16[256,2048]{1,0:T(8,128)(2,1)S(1)}, u32[]{:S(2)}, u32[]{:S(2)}) collective-permute-start(bf16[256,2048]{1,0:T(8,128)(2,1)} %gate.7.refs_0_), channel_id=1, source_target_pairs={{0,2},{1,3},{2,0},{3,1},{4,6},{5,7},{6,4},{7,5},{8,10},{9,11},{10,... | collective-permute-start | bytes 3145736 | tf_op jit(solution)/shard_map/ppermute | solution.py:238
  109.4 24.8 %collective-permute-start.20 = (bf16[256,2048]{1,0:T(8,128)(2,1)}, bf16[256,2048]{1,0:T(8,128)(2,1)S(1)}, u32[]{:S(2)}, u32[]{:S(2)}) collective-permute-start(bf16[256,2048]{1,0:T(8,128)(2,1)} %gate.7.refs_0_), channel_id=1, source_target_pairs={{0,4},{1,5},{2,6},{3,7},{4,0},{5,1},{6,2},{7,3},{8,12},{9,13},{10,... | collective-permute-start | bytes 3145736 | tf_op jit(solution)/shard_map/ppermute | solution.py:238
  143.4 112.9 %all-gather.8.cloned.1.call-start = ((), (), s32[]{:S(2)}) async-start(), calls=%async_computation.8 | async-start | bytes 5242880 | tf_op jit(solution)/shard_map/all_gather | solution.py:463
  174.8 228.0 %reduce-scatter.3.cloned.1.call-start = ((), (), s32[]{:S(2)}) async-start(), calls=%async_computation.9 | async-start | bytes 10485760 | tf_op jit(solution)/shard_map/reduce_scatter | solution.py:483
  237.4 269.6 %reduce-scatter.5.cloned.1.call-start = ((), (), s32[]{:S(2)}) async-start(), calls=%async_computation.10 | async-start | bytes 5242880 | tf_op jit(solution)/shard_map/reduce_scatter | solution.py:511
  353.4 50.0 %collective-permute-start.24 = (bf16[4,256,2048]{2,1,0:T(8,128)(2,1)}, bf16[4,256,2048]{2,1,0:T(8,128)(2,1)}, u32[]{:S(2)}, u32[]{:S(2)}) collective-permute-start(bf16[4,256,2048]{2,1,0:T(8,128)(2,1)} %get-tuple-element.34), channel_id=1, source_target_pairs={{0,1},{1,0},{2,3},{3,2},{4,5},{5,4},{6,7},{7,6},{8,9},{9,8},{10,11... | collective-permute-start | bytes 12582920 | tf_op jit(solution)/shard_map/ppermute | solution.py:238
  375.4 39.4 %collective-permute-start.12 = (bf16[4,256,2048]{2,1,0:T(8,128)(2,1)}, bf16[4,256,2048]{2,1,0:T(8,128)(2,1)}, u32[]{:S(2)}, u32[]{:S(2)}) collective-permute-start(bf16[4,256,2048]{2,1,0:T(8,128)(2,1)} %get-tuple-element.28), channel_id=1, source_target_pairs={{0,1},{1,0},{2,3},{3,2},{4,5},{5,4},{6,7},{7,6},{8,9},{9,8},{10,11... | collective-permute-start | bytes 12582920 | tf_op jit(solution)/shard_map/ppermute | solution.py:238
  411.6 26.4 %collective-permute-start.27 = (bf16[2,256,1024]{2,1,0:T(8,128)(2,1)}, bf16[2,256,1024]{2,1,0:T(8,128)(2,1)}, u32[]{:S(2)}, u32[]{:S(2)}) collective-permute-start(bf16[2,256,1024]{2,1,0:T(8,128)(2,1)} %fusion.23), channel_id=1, source_target_pairs={{0,4},{1,5},{2,6},{3,7},{4,0},{5,1},{6,2},{7,3},{8,12},{9,13},{10,... | collective-permute-start | bytes 3145736 | tf_op jit(solution)/shard_map/ppermute | solution.py:238
  413.2 27.9 %collective-permute-start.25 = (bf16[2,256,1024]{2,1,0:T(8,128)(2,1)S(1)}, bf16[2,256,1024]{2,1,0:T(8,128)(2,1)}, u32[]{:S(2)}, u32[]{:S(2)}) collective-permute-start(bf16[2,256,1024]{2,1,0:T(8,128)(2,1)S(1)} %fusion.25), channel_id=1, source_target_pairs={{0,2},{1,3},{2,0},{3,1},{4,6},{5,7},{6,4},{7,5},{8,10},{9,11},{10,... | collective-permute-start | bytes 3145736 | tf_op jit(solution)/shard_map/ppermute | solution.py:238
  420.6 39.8 %collective-permute-start.15 = (bf16[2,256,1024]{2,1,0:T(8,128)(2,1)S(1)}, bf16[2,256,1024]{2,1,0:T(8,128)(2,1)S(1)}, u32[]{:S(2)}, u32[]{:S(2)}) collective-permute-start(bf16[2,256,1024]{2,1,0:T(8,128)(2,1)S(1)} %fusion.22), channel_id=1, source_target_pairs={{0,4},{1,5},{2,6},{3,7},{4,0},{5,1},{6,2},{7,3},{8,12},{9,13},{10,... | collective-permute-start | bytes 3145736 | tf_op jit(solution)/shard_map/ppermute | solution.py:238
  423.2 39.2 %collective-permute-start.13 = (bf16[2,256,1024]{2,1,0:T(8,128)(2,1)S(1)}, bf16[2,256,1024]{2,1,0:T(8,128)(2,1)S(1)}, u32[]{:S(2)}, u32[]{:S(2)}) collective-permute-start(bf16[2,256,1024]{2,1,0:T(8,128)(2,1)S(1)} %fusion.24), channel_id=1, source_target_pairs={{0,2},{1,3},{2,0},{3,1},{4,6},{5,7},{6,4},{7,5},{8,10},{9,11},{10,... | collective-permute-start | bytes 3145736 | tf_op jit(solution)/shard_map/ppermute | solution.py:238
  439.7 33.4 %collective-permute-start.28 = (bf16[256,1024]{1,0:T(8,128)(2,1)S(1)}, bf16[256,1024]{1,0:T(8,128)(2,1)S(1)}, u32[]{:S(2)}, u32[]{:S(2)}) collective-permute-start(bf16[256,1024]{1,0:T(8,128)(2,1)S(1)} %fusion.29), channel_id=1, source_target_pairs={{0,2},{1,3},{2,0},{3,1},{4,6},{5,7},{6,4},{7,5},{8,10},{9,11},{10,... | collective-permute-start | bytes 1572872 | tf_op jit(solution)/shard_map/ppermute | solution.py:238
  442.8 30.5 %collective-permute-start.26 = (bf16[256,1024]{1,0:T(8,128)(2,1)S(1)}, bf16[256,1024]{1,0:T(8,128)(2,1)S(1)}, u32[]{:S(2)}, u32[]{:S(2)}) collective-permute-start(bf16[256,1024]{1,0:T(8,128)(2,1)S(1)} %fusion.28), channel_id=1, source_target_pairs={{0,4},{1,5},{2,6},{3,7},{4,0},{5,1},{6,2},{7,3},{8,12},{9,13},{10,... | collective-permute-start | bytes 1572872 | tf_op jit(solution)/shard_map/ppermute | solution.py:238
  460.9 21.8 %collective-permute-start.16 = (bf16[256,1024]{1,0:T(8,128)(2,1)S(1)}, bf16[256,1024]{1,0:T(8,128)(2,1)S(1)}, u32[]{:S(2)}, u32[]{:S(2)}) collective-permute-start(bf16[256,1024]{1,0:T(8,128)(2,1)S(1)} %fusion.27), channel_id=1, source_target_pairs={{0,2},{1,3},{2,0},{3,1},{4,6},{5,7},{6,4},{7,5},{8,10},{9,11},{10,... | collective-permute-start | bytes 1572872 | tf_op jit(solution)/shard_map/ppermute | solution.py:238
  (70 other events, 1196.5 us)
Sparse Core Ops, SparseCore 0:
  9.7 83.5 all-gather.3
  95.4 79.2 all-gather.5
  176.9 79.2 all-gather.7
  258.4 144.3 reduce-scatter.2
  404.9 77.4 reduce-scatter.4

commit v3 on v2

--- a/solution.py
+++ b/solution.py
@@ -510,10 +510,11 @@
         grad_wout = lax.psum_scatter(spread, BOTH, scatter_dimension=0, tiled=True).astype(f32)
     first = lax.psum_scatter(gate(term_a, both), "fsdp", scatter_dimension=0, tiled=True)
 
+    traded = trade(grad_wfc1)
     if groups == 8:
         mixed = back_product(attn, wout, up, wfc2, groups)
         *d_normed, sums = back_product(d_proj, weights_a, d_pre, wfc1, groups, hat_all)
-        mixed = sum_end(*sum_start(*sum_sends(sum_core(*mixed))))
+        mixed = sum_end(*sum_start(*sum_sends(sum_core(mixed[0], gate(mixed[1], traded)))))
         d_normed = sum_end(*sum_start(*sum_sends(sum_core(*d_normed))))
     else:
         mixed = dot(attn, wout, 0, 0) + dot(up, wfc2, 0, 0)
@@ -523,7 +524,6 @@
             lax.psum_scatter(v.astype(bf16), "seq", scatter_dimension=0, tiled=True).astype(f32)
             for v in (d_normed, mixed)
         )
-    traded = trade(grad_wfc1)
     rows_wfc1 = to_rows(traded, groups, shards)
     grad_wfc2 = grad_wfc2.astype(f32)
 
@@ -548,7 +548,7 @@
         at += count
     grad_gain, grad_shift, grad_bqk, grad_bv, grad_bout, grad_bfc1 = vector_grads
 
-    first = gate(first, d_normed, mixed, traded, summed)
+    first = gate(first, d_normed)
     if whole_heads:
         grad_wout = first[:, inner:].reshape(out_rows, width).astype(f32)
     grad_wqkv = to_rows(trade(first[:, :inner]), groups, 3 * heads)

time: 541 us -> 537 us (level)
  waiting for transfers between devices: 192 us -> 175 us
  local copies, waits for them, and re-layouts: 28.5 us -> 37.5 us
    ppermute x32, waiting for transfers between devices: 112 us -> 103 us  [swap(): return lax.ppermute(value, axes, [(i, i ^ bit) for i in range(size)])]
    all_to_all x4, waiting for transfers between devices: 19 us -> 11.8 us  [trade(): lax.all_to_all(values, 'seq', split_axis=0, concat_axis=0, tiled=True)]
    unnamed x104 -> x94, local copies, waits for them, and re-layouts: 12.9 us -> 9.49 us
  transfers between devices with their start and end apart: 43 -> 43, of which waited for: 21 -> 20; matrix products, arithmetic and copies ran while one was open for 28% -> 31% of each run, Pallas kernels for 21% -> 21%
where the time goes in v3:
time: 537 us; the launch traced here: 531 us
  waiting for transfers between devices  175 us (33%)
  Pallas kernels  115 us (21%)
  matrix products  89.5 us (17%)
  starting transfers between devices  50.9 us (9%)
  other arithmetic  48.1 us (9%)
  local copies, waits for them, and re-layouts  37.5 us (7%)
  between operations  15.2 us (3%)
    ppermute x32, waiting for transfers between devices, swap(): return lax.ppermute(value, axes, [(i, i ^ bit) for i in range(size)])  103 us
    dot_general x8, matrix products, dot(): lax.dot_general(a, b, (((ca,), (cb,)), ((), ())), preferred_element_type=...  89.5 us
    pallas_call x2, Pallas kernels, back_product(): pl.pallas_call(functools.partial(back_kernel, turned), grid_spec=pltpu.Pr...  43.5 us
    ppermute x32, starting transfers between devices, swap(): return lax.ppermute(value, axes, [(i, i ^ bit) for i in range(size)])  33.5 us
    pallas_call x1, Pallas kernels, attend_backward(): pl.pallas_call(functools.partial(backward_kernel, block), grid=(heads,),...  28 us
    all_gather x1, waiting for transfers between devices, local(): wfc2 = lax.all_gather(second_feed_weight, 'fsdp', axis=0, tiled=True)  21.8 us
    pallas_call x2, Pallas kernels, put_in_order(): pl.pallas_call(functools.partial(pieces_kernel, bool(vectors)), grid_spec...  21 us
    all_gather x1, waiting for transfers between devices, local(): first = lax.all_gather(gate(first, wfc1), 'fsdp', axis=0, tiled=True)  18.8 us
  transfers between devices with their start and end apart: 43, of which 20 were waited for; matrix products, arithmetic and copies ran while one was open for 31% of the time, Pallas kernels for 21%

profile of v3, /device:TPU:0, one launch (start us, length us, event | category | flops | bytes accessed | tf_op | source)
XLA Modules:
  0.0 530.8 jit_solution(13513127272087186921)
XLA Ops:
  12.5 21.9 %collective-permute-done.1.refs_2_ = bf16[256,2048]{1,0:T(8,128)(2,1)S(1)} collective-permute-done((bf16[256,2048]{1,0:T(8,128)(2,1)}, bf16[256,2048]{1,0:T(8,128)(2,1)S(1)}, u32[]{:S(2)}, u32[]{:S(2)}) %collective-permute-start.1) | collective-permute-done | bytes 1048608 | tf_op jit(solution)/shard_map/ppermute | solution.py:238
  55.6 11.9 %collective-permute-done.10 = bf16[2,4,704]{2,1,0:T(4,128)(2,1)S(1)} collective-permute-done((bf16[2,4,704]{2,1,0:T(4,128)(2,1)S(1)}, bf16[2,4,704]{2,1,0:T(4,128)(2,1)S(1)}, u32[]{:S(2)}, u32[]{:S(2)}) %collective-permute-start.10) | collective-permute-done | bytes 11296 | tf_op jit(solution)/shard_map/ppermute | solution.py:238
  71.5 21.8 %all-gather.4.cloned.1.call-done.refs_1_.wb_ref = bf16[1024,2048]{1,0:T(8,128)(2,1)} async-done(((bf16[256,2048]{1,0:T(8,128)(2,1)}), bf16[1024,2048]{1,0:T(8,128)(2,1)}) %all-gather.4.cloned.1.call-update) | async-done | bytes 4194320 | tf_op jit(solution)/shard_map/all_gather | solution.py:457
  94.2 12.9 %put_in_order.2 = (bf16[2048,2048]{1,0:T(8,128)(2,1)}, bf16[2048,2048]{1,0:T(8,128)(2,1)}) custom-call(s32[8]{0:T(128)S(1)} %stack.44.order_ref, bf16[256,2048]{1,0:T(8,128)(2,1)S(1)} %bitcast.128, bf16[256,2048]{1,0:T(8,128)(2,1)} %collective-permute-done.refs_1_, bf16[256,2048]{1,0:T(8,128)(2,1)S(1)} %collective-permute-done.1.refs_2_, ...), custom_call_target="tpu_custom_call" | custom-call | flops 11500000256 | bytes 1 | tf_op jit(solution)/shard_map/put_in_order/pallas_call | solution.py:316
  115.7 17.8 %collective-permute-done.13.refs_2_ = bf16[256,2048]{1,0:T(8,128)(2,1)S(1)} collective-permute-done((bf16[256,2048]{1,0:T(8,128)(2,1)}, bf16[256,2048]{1,0:T(8,128)(2,1)S(1)}, u32[]{:S(2)}, u32[]{:S(2)}) %collective-permute-start.13) | collective-permute-done | bytes 1048608 | tf_op jit(solution)/shard_map/ppermute | solution.py:238
  140.9 11.4 %collective-permute-done.17.refs_6_ = bf16[256,2048]{1,0:T(8,128)(2,1)} collective-permute-done((bf16[256,2048]{1,0:T(8,128)(2,1)S(1)}, bf16[256,2048]{1,0:T(8,128)(2,1)}, u32[]{:S(2)}, u32[]{:S(2)}) %collective-permute-start.17) | collective-permute-done | bytes 1048608 | tf_op jit(solution)/shard_map/ppermute | solution.py:284
  160.0 8.1 %put_in_order.3 = bf16[2048,2048]{1,0:T(8,128)(2,1)} custom-call(s32[8]{0:T(128)S(1)} %stack.44.order_ref, bf16[256,2048]{1,0:T(8,128)(2,1)S(1)} %copy-done.4, bf16[256,2048]{1,0:T(8,128)(2,1)} %collective-permute-done.12.refs_1_, bf16[256,2048]{1,0:T(8,128)(2,1)S(1)} %collective-permute-done.13.refs_2_, bf16[256,2048]{1,0:T(8,128)(2,1)} %collective-permute-done.14.refs_3_, ...), custom_call_target="tpu_custom_call" | custom-call | flops 11500000256 | bytes 1 | tf_op jit(solution)/shard_map/put_in_order/pallas_call | solution.py:316
  168.2 6.6 %all-gather.6.cloned.1.call-done.refs_1_.wb_ref = bf16[2048,1024]{1,0:T(8,128)(2,1)} async-done(((bf16[512,1024]{1,0:T(8,128)(2,1)}), bf16[2048,1024]{1,0:T(8,128)(2,1)}) %all-gather.6.cloned.1.call-update) | async-done | bytes 4194320 | tf_op jit(solution)/shard_map/all_gather | solution.py:459
  175.0 16.7 %multiply_convert_fusion = (bf16[1024,2048]{1,0:T(8,128)(2,1)}, f32[1024,2048]{1,0:T(8,128)S(1)}) fusion(f32[1024]{0:T(1024)S(1)} %bitcast.143, bf16[2048,1024]{1,0:T(8,128)(2,1)} %all-gather.6.cloned.1.call-done.refs_1_.wb_ref, bf16[2048,2048]{1,0:T(8,128)(2,1)} %get-tuple-element.25.refs_1_), kind=kOutput, calls=%fused_computation.13 | convolution fusion | flops 8610906112 | bytes 25169920 | tf_op jit(solution)/shard_map/dot_general | solution.py:20
  191.7 15.2 %convert_reduce_fusion = (f32[1024]{0:T(1024)S(1)}, bf16[1024,2048]{1,0:T(8,128)(2,1)}) fusion(f32[1024,2048]{1,0:T(8,128)S(1)} %get-tuple-element.73, f32[1024]{0:T(1024)S(1)} %bitcast.144, bf16[2048,2048]{1,0:T(8,128)(2,1)} %put_in_order.3, bf16[1024,2048]{1,0:T(8,128)(2,1)S(1)} %copy-done.25), kind=kOutput, calls=%fused_computation.10 | convolution fusion | flops 8636070912 | bytes 25174016 | tf_op jit(solution)/shard_map/dot_general | solution.py:20
  206.9 12.8 %convolution_convert_fusion.1 = bf16[2048,1024]{1,0:T(8,128)(2,1)S(1)} fusion(bf16[2048,2048]{1,0:T(8,128)(2,1)} %get-tuple-element.25.refs_1_, bf16[1024,2048]{1,0:T(8,128)(2,1)} %get-tuple-element.75.b_ref), kind=kOutput, calls=%fused_computation.16 | convolution fusion | flops 8592031744 | bytes 16777216 | tf_op jit(solution)/shard_map/dot_general | solution.py:20
  221.9 11.2 %convolution_convert_fusion = bf16[1024,2048]{1,0:T(8,128)(2,1)S(1)} fusion(bf16[1024,2048]{1,0:T(8,128)(2,1)S(1)} %copy-done.44, bf16[2048,2048]{1,0:T(8,128)(2,1)} %put_in_order.3), kind=kOutput, calls=%fused_computation.15 | convolution fusion | flops 8592031744 | bytes 16777216 | tf_op jit(solution)/shard_map/dot_general | solution.py:20
  237.5 18.8 %all-gather.8.cloned.1.call-done.wa_ref = bf16[2048,1024]{1,0:T(8,128)(2,1)} async-done(((bf16[512,1024]{1,0:T(8,128)(2,1)}), bf16[2048,1024]{1,0:T(8,128)(2,1)}) %all-gather.8.cloned.1.call-update) | async-done | bytes 4194320 | tf_op jit(solution)/shard_map/all_gather | solution.py:463
  258.5 6.2 %convolution_convert_fusion.4.g_ref = bf16[256,2048]{1,0:T(8,128)(2,1)S(1)} fusion(bf16[256,2048]{1,0:T(8,128)(2,1)S(1)} %reshape.272.wa_ref, bf16[2048,2048]{1,0:T(8,128)(2,1)} %put_in_order.3), kind=kOutput, calls=%fused_computation.25 | convolution fusion | flops 2148007936 | bytes 10485760 | tf_op jit(solution)/shard_map/dot_general | solution.py:20
  264.7 11.1 %convolution_add_fusion.q_ref.k_ref.v_ref = f32[768,2048]{1,0:T(8,128)} fusion(bf16[2048,2048]{1,0:T(8,128)(2,1)} %get-tuple-element.25.refs_1_, bf16[2048,1024]{1,0:T(8,128)(2,1)S(1)} %copy-done.27, f32[768]{0:T(1024)S(1)} %add.178), kind=kOutput, calls=%fused_computation.17 | convolution fusion | flops 6444023808 | bytes 17829888 | tf_op jit(solution)/shard_map/dot_general | solution.py:20
  275.8 17.2 %attend_forward.1 = (bf16[256,2048]{1,0:T(8,128)(2,1)S(1)}, f32[4,1,2048]{2,1,0:T(1,128)S(1)}, bf16[3,4,64,2048]{3,2,1,0:T(8,128)(2,1)S(1)}) custom-call(f32[768,2048]{1,0:T(8,128)} %convolution_add_fusion.q_ref.k_ref.v_ref, f32[768,2048]{1,0:T(8,128)} %convolution_add_fusion.q_ref.k_ref.v_ref, f32[768,2048]{1,0:T(8,128)} %convolution_add_fusion.q_ref.k_ref.v_ref, ...), custom_call_target="tpu_custom_call" | custom-call | flops 19549999104 | bytes 1 | tf_op jit(solution)/shard_map/attend_forward/pallas_call | solution.py:72
  294.6 28.0 %attend_backward.1 = (bf16[3,4,64,2048]{3,2,1,0:T(8,128)(2,1)S(1)}, f32[3,4,64,128]{3,2,1,0:T(8,128)S(1)}) custom-call(bf16[3,4,64,2048]{3,2,1,0:T(8,128)(2,1)} %copy-done.11, bf16[256,2048]{1,0:T(8,128)(2,1)S(1)} %get-tuple-element.26.a_ref.o_ref, bf16[256,2048]{1,0:T(8,128)(2,1)S(1)} %convolution_convert_fusion.4.g_ref, ...), custom_call_target="tpu_custom_call" | custom-call | flops 32199999488 | bytes 1 | tf_op jit(solution)/shard_map/attend_backward/pallas_call | solution.py:142
  324.3 26.7 %back_product.3 = (bf16[4,256,2048]{2,1,0:T(8,128)(2,1)}, bf16[4,256,2048]{2,1,0:T(8,128)(2,1)}, f32[8,2048]{1,0:T(8,128)}) custom-call(s32[1]{0:T(128)} %bitcast.core_ref, bf16[768,2048]{1,0:T(8,128)(2,1)} %bitcast.130, bf16[2048,1024]{1,0:T(8,128)(2,1)} %all-gather.8.cloned.1.call-done.wa_ref, bf16[1024,2048]{1,0:T(8,128)(2,1)} %get-tuple-element.75.b_ref, ...), custom_call_target="tpu_custom_call" | custom-call | flops 31050000384 | bytes 1 | tf_op jit(solution)/shard_map/back_product/pallas_call | solution.py:197
  359.7 10.6 %convolution_convert_fusion.2 = bf16[2048,768]{1,0:T(8,128)(2,1)} fusion(bf16[2048,2048]{1,0:T(8,128)(2,1)} %get-tuple-element.25.refs_1_, bf16[768,2048]{1,0:T(8,128)(2,1)S(1)} %bitcast.131), kind=kOutput, calls=%fused_computation.18 | convolution fusion | flops 6444023808 | bytes 14680064 | tf_op jit(solution)/shard_map/dot_general | solution.py:20
  370.9 16.8 %back_product.2 = (bf16[4,256,2048]{2,1,0:T(8,128)(2,1)}, bf16[4,256,2048]{2,1,0:T(8,128)(2,1)}) custom-call(s32[1]{0:T(128)} %bitcast.core_ref, bf16[256,2048]{1,0:T(8,128)(2,1)} %copy-done.9, bf16[256,2048]{1,0:T(8,128)(2,1)} %copy-done.26, bf16[1024,2048]{1,0:T(8,128)(2,1)} %get-tuple-element.72.b_ref, ...), custom_call_target="tpu_custom_call" | custom-call | flops 19549999104 | bytes 1 | tf_op jit(solution)/shard_map/back_product/pallas_call | solution.py:197
  421.7 15.6 %collective-permute-done.27 = bf16[2,256,1024]{2,1,0:T(8,128)(2,1)} collective-permute-done((bf16[2,256,1024]{2,1,0:T(8,128)(2,1)}, bf16[2,256,1024]{2,1,0:T(8,128)(2,1)}, u32[]{:S(2)}, u32[]{:S(2)}) %collective-permute-start.27) | collective-permute-done | bytes 1048608 | tf_op jit(solution)/shard_map/ppermute | solution.py:238
  469.2 14.6 %collective-permute-done.22 = bf16[2,256,1024]{2,1,0:T(8,128)(2,1)S(1)} collective-permute-done((bf16[2,256,1024]{2,1,0:T(8,128)(2,1)S(1)}, bf16[2,256,1024]{2,1,0:T(8,128)(2,1)S(1)}, u32[]{:S(2)}, u32[]{:S(2)}) %collective-permute-start.22) | collective-permute-done | bytes 1048608 | tf_op jit(solution)/shard_map/ppermute | solution.py:238
  494.1 6.3 %collective-permute-done.23 = bf16[256,1024]{1,0:T(8,128)(2,1)S(1)} collective-permute-done((bf16[256,1024]{1,0:T(8,128)(2,1)S(1)}, bf16[256,1024]{1,0:T(8,128)(2,1)S(1)}, u32[]{:S(2)}, u32[]{:S(2)}) %collective-permute-start.23) | collective-permute-done | bytes 524320 | tf_op jit(solution)/shard_map/ppermute | solution.py:238
  515.7 6.2 %all-to-all-done.3.g_ref = bf16[8,64,768]{2,1,0:T(8,128)(2,1)S(1)} async-done(((bf16[8,64,768]{2,1,0:T(8,128)(2,1)}), bf16[8,64,768]{2,1,0:T(8,128)(2,1)S(1)}, u32[]{:S(2)}, u32[]{:S(2)}) %all-to-all-start.3) | async-done | bytes 786464 | tf_op jit(solution)/shard_map/all_to_all | solution.py:401
  (290 shorter events, 169.3 us)
Async XLA Ops:
  7.3 86.0 %all-gather.4.cloned.1.call-start = ((), (), s32[]{:S(2)}) async-start(), calls=%async_computation.6 | async-start | bytes 5242880 | tf_op jit(solution)/shard_map/all_gather | solution.py:457
  8.0 26.4 %collective-permute-start.1 = (bf16[256,2048]{1,0:T(8,128)(2,1)}, bf16[256,2048]{1,0:T(8,128)(2,1)S(1)}, u32[]{:S(2)}, u32[]{:S(2)}) collective-permute-start(bf16[256,2048]{1,0:T(8,128)(2,1)} %bitcast.125), channel_id=1, source_target_pairs={{0,2},{1,3},{2,0},{3,1},{4,6},{5,7},{6,4},{7,5},{8,10},{9,11},{10,... | collective-permute-start | bytes 3145736 | tf_op jit(solution)/shard_map/ppermute | solution.py:238
  11.0 24.9 %collective-permute-start.3 = (bf16[256,2048]{1,0:T(8,128)(2,1)}, bf16[256,2048]{1,0:T(8,128)(2,1)}, u32[]{:S(2)}, u32[]{:S(2)}) collective-permute-start(bf16[256,2048]{1,0:T(8,128)(2,1)} %bitcast.126), channel_id=1, source_target_pairs={{0,4},{1,5},{2,6},{3,7},{4,0},{5,1},{6,2},{7,3},{8,12},{9,13},{10,... | collective-permute-start | bytes 3145736 | tf_op jit(solution)/shard_map/ppermute | solution.py:238
  47.5 46.6 %collective-permute-start = (bf16[256,2048]{1,0:T(8,128)(2,1)S(1)}, bf16[256,2048]{1,0:T(8,128)(2,1)}, u32[]{:S(2)}, u32[]{:S(2)}) collective-permute-start(bf16[256,2048]{1,0:T(8,128)(2,1)S(1)} %bitcast.127), channel_id=1, source_target_pairs={{0,1},{1,0},{2,3},{3,2},{4,5},{5,4},{6,7},{7,6},{8,9},{9,8},{10,11... | collective-permute-start | bytes 3145736 | tf_op jit(solution)/shard_map/ppermute | solution.py:238
  49.1 22.4 %all-to-all-start.1 = ((bf16[8,64,1024]{2,1,0:T(8,128)(2,1)}), bf16[8,64,1024]{2,1,0:T(8,128)(2,1)S(1)}, u32[]{:S(2)}, u32[]{:S(2)}) async-start(bf16[8,64,1024]{2,1,0:T(8,128)(2,1)} %regroup.5), calls=%async_computation.1 | async-start | bytes 2097152 | tf_op jit(solution)/shard_map/all_to_all | solution.py:401
  52.7 122.0 %all-gather.6.cloned.1.call-start = ((), (), s32[]{:S(2)}) async-start(), calls=%async_computation.7 | async-start | bytes 5242880 | tf_op jit(solution)/shard_map/all_gather | solution.py:459
  52.8 41.4 %collective-permute-start.2 = (bf16[256,2048]{1,0:T(8,128)(2,1)S(1)}, bf16[256,2048]{1,0:T(8,128)(2,1)}, u32[]{:S(2)}, u32[]{:S(2)}) collective-permute-start(bf16[256,2048]{1,0:T(8,128)(2,1)S(1)} %collective-permute-done.1.refs_2_), channel_id=1, source_target_pairs={{0,1},{1,0},{2,3},{3,2},{4,5},{5,4},{6,7},{7,6},{8,9},{9,8},{10,11... | collective-permute-start | bytes 3145736 | tf_op jit(solution)/shard_map/ppermute | solution.py:238
  53.3 40.9 %collective-permute-start.4 = (bf16[256,2048]{1,0:T(8,128)(2,1)}, bf16[256,2048]{1,0:T(8,128)(2,1)}, u32[]{:S(2)}, u32[]{:S(2)}) collective-permute-start(bf16[256,2048]{1,0:T(8,128)(2,1)} %collective-permute-done.3.refs_4_), channel_id=1, source_target_pairs={{0,1},{1,0},{2,3},{3,2},{4,5},{5,4},{6,7},{7,6},{8,9},{9,8},{10,11... | collective-permute-start | bytes 3145736 | tf_op jit(solution)/shard_map/ppermute | solution.py:238
  53.4 40.8 %collective-permute-start.6 = (bf16[256,2048]{1,0:T(8,128)(2,1)}, bf16[256,2048]{1,0:T(8,128)(2,1)}, u32[]{:S(2)}, u32[]{:S(2)}) collective-permute-start(bf16[256,2048]{1,0:T(8,128)(2,1)} %collective-permute-done.5.refs_6_), channel_id=1, source_target_pairs={{0,1},{1,0},{2,3},{3,2},{4,5},{5,4},{6,7},{7,6},{8,9},{9,8},{10,11... | collective-permute-start | bytes 3145736 | tf_op jit(solution)/shard_map/ppermute | solution.py:238
  107.1 26.3 %collective-permute-start.13 = (bf16[256,2048]{1,0:T(8,128)(2,1)}, bf16[256,2048]{1,0:T(8,128)(2,1)S(1)}, u32[]{:S(2)}, u32[]{:S(2)}) collective-permute-start(bf16[256,2048]{1,0:T(8,128)(2,1)} %gate.8.refs_0_), channel_id=1, source_target_pairs={{0,2},{1,3},{2,0},{3,1},{4,6},{5,7},{6,4},{7,5},{8,10},{9,11},{10,... | collective-permute-start | bytes 3145736 | tf_op jit(solution)/shard_map/ppermute | solution.py:238
  108.7 27.3 %collective-permute-start.15 = (bf16[256,2048]{1,0:T(8,128)(2,1)}, bf16[256,2048]{1,0:T(8,128)(2,1)}, u32[]{:S(2)}, u32[]{:S(2)}) collective-permute-start(bf16[256,2048]{1,0:T(8,128)(2,1)} %gate.8.refs_0_), channel_id=1, source_target_pairs={{0,4},{1,5},{2,6},{3,7},{4,0},{5,1},{6,2},{7,3},{8,12},{9,13},{10,... | collective-permute-start | bytes 3145736 | tf_op jit(solution)/shard_map/ppermute | solution.py:238
  111.3 46.5 %all-to-all-start = ((bf16[8,64,768]{2,1,0:T(8,128)(2,1)}), bf16[8,64,768]{2,1,0:T(8,128)(2,1)}, u32[]{:S(2)}, u32[]{:S(2)}) async-start(bf16[8,64,768]{2,1,0:T(8,128)(2,1)} %regroup.4), calls=%async_computation | async-start | bytes 1572864 | tf_op jit(solution)/shard_map/all_to_all | solution.py:401
  115.6 140.6 %all-gather.8.cloned.1.call-start = ((), (), s32[]{:S(2)}) async-start(), calls=%async_computation.8 | async-start | bytes 5242880 | tf_op jit(solution)/shard_map/all_gather | solution.py:463
  174.8 227.9 %reduce-scatter.3.cloned.1.call-start = ((), (), s32[]{:S(2)}) async-start(), calls=%async_computation.9 | async-start | bytes 10485760 | tf_op jit(solution)/shard_map/reduce_scatter | solution.py:483
  236.7 266.9 %reduce-scatter.5.cloned.1.call-start = ((), (), s32[]{:S(2)}) async-start(), calls=%async_computation.10 | async-start | bytes 5242880 | tf_op jit(solution)/shard_map/reduce_scatter | solution.py:511
  370.2 32.6 %collective-permute-start.24 = (bf16[4,256,2048]{2,1,0:T(8,128)(2,1)}, bf16[4,256,2048]{2,1,0:T(8,128)(2,1)}, u32[]{:S(2)}, u32[]{:S(2)}) collective-permute-start(bf16[4,256,2048]{2,1,0:T(8,128)(2,1)} %get-tuple-element.34), channel_id=1, source_target_pairs={{0,1},{1,0},{2,3},{3,2},{4,5},{5,4},{6,7},{7,6},{8,9},{9,8},{10,11... | collective-permute-start | bytes 12582920 | tf_op jit(solution)/shard_map/ppermute | solution.py:238
  395.4 57.8 %collective-permute-start.19 = (bf16[4,256,2048]{2,1,0:T(8,128)(2,1)}, bf16[4,256,2048]{2,1,0:T(8,128)(2,1)}, u32[]{:S(2)}, u32[]{:S(2)}) collective-permute-start(bf16[4,256,2048]{2,1,0:T(8,128)(2,1)} %get-tuple-element.28), channel_id=1, source_target_pairs={{0,1},{1,0},{2,3},{3,2},{4,5},{5,4},{6,7},{7,6},{8,9},{9,8},{10,11... | collective-permute-start | bytes 12582920 | tf_op jit(solution)/shard_map/ppermute | solution.py:238
  411.1 26.3 %collective-permute-start.27 = (bf16[2,256,1024]{2,1,0:T(8,128)(2,1)}, bf16[2,256,1024]{2,1,0:T(8,128)(2,1)}, u32[]{:S(2)}, u32[]{:S(2)}) collective-permute-start(bf16[2,256,1024]{2,1,0:T(8,128)(2,1)} %fusion.24), channel_id=1, source_target_pairs={{0,4},{1,5},{2,6},{3,7},{4,0},{5,1},{6,2},{7,3},{8,12},{9,13},{10,... | collective-permute-start | bytes 3145736 | tf_op jit(solution)/shard_map/ppermute | solution.py:238
  414.5 27.5 %collective-permute-start.25 = (bf16[2,256,1024]{2,1,0:T(8,128)(2,1)}, bf16[2,256,1024]{2,1,0:T(8,128)(2,1)}, u32[]{:S(2)}, u32[]{:S(2)}) collective-permute-start(bf16[2,256,1024]{2,1,0:T(8,128)(2,1)} %fusion.25), channel_id=1, source_target_pairs={{0,2},{1,3},{2,0},{3,1},{4,6},{5,7},{6,4},{7,5},{8,10},{9,11},{10,... | collective-permute-start | bytes 3145736 | tf_op jit(solution)/shard_map/ppermute | solution.py:238
  417.1 35.2 %all-to-all-start.2 = ((bf16[8,64,1024]{2,1,0:T(8,128)(2,1)}), bf16[8,64,1024]{2,1,0:T(8,128)(2,1)S(1)}, u32[]{:S(2)}, u32[]{:S(2)}) async-start(bf16[8,64,1024]{2,1,0:T(8,128)(2,1)} %bitcast.140), calls=%async_computation.3 | async-start | bytes 2097152 | tf_op jit(solution)/shard_map/all_to_all | solution.py:401
  440.5 22.4 %collective-permute-start.28 = (bf16[256,1024]{1,0:T(8,128)(2,1)}, bf16[256,1024]{1,0:T(8,128)(2,1)}, u32[]{:S(2)}, u32[]{:S(2)}) collective-permute-start(bf16[256,1024]{1,0:T(8,128)(2,1)} %fusion.31), channel_id=1, source_target_pairs={{0,2},{1,3},{2,0},{3,1},{4,6},{5,7},{6,4},{7,5},{8,10},{9,11},{10,... | collective-permute-start | bytes 1572872 | tf_op jit(solution)/shard_map/ppermute | solution.py:238
  445.2 20.7 %collective-permute-start.26 = (bf16[256,1024]{1,0:T(8,128)(2,1)}, bf16[256,1024]{1,0:T(8,128)(2,1)}, u32[]{:S(2)}, u32[]{:S(2)}) collective-permute-start(bf16[256,1024]{1,0:T(8,128)(2,1)} %fusion.30), channel_id=1, source_target_pairs={{0,4},{1,5},{2,6},{3,7},{4,0},{5,1},{6,2},{7,3},{8,12},{9,13},{10,... | collective-permute-start | bytes 1572872 | tf_op jit(solution)/shard_map/ppermute | solution.py:238
  460.5 23.3 %collective-permute-start.22 = (bf16[2,256,1024]{2,1,0:T(8,128)(2,1)S(1)}, bf16[2,256,1024]{2,1,0:T(8,128)(2,1)S(1)}, u32[]{:S(2)}, u32[]{:S(2)}) collective-permute-start(bf16[2,256,1024]{2,1,0:T(8,128)(2,1)S(1)} %fusion.23), channel_id=1, source_target_pairs={{0,4},{1,5},{2,6},{3,7},{4,0},{5,1},{6,2},{7,3},{8,12},{9,13},{10,... | collective-permute-start | bytes 3145736 | tf_op jit(solution)/shard_map/ppermute | solution.py:238
  464.3 26.1 %collective-permute-start.20 = (bf16[2,256,1024]{2,1,0:T(8,128)(2,1)S(1)}, bf16[2,256,1024]{2,1,0:T(8,128)(2,1)S(1)}, u32[]{:S(2)}, u32[]{:S(2)}) collective-permute-start(bf16[2,256,1024]{2,1,0:T(8,128)(2,1)S(1)} %fusion.22), channel_id=1, source_target_pairs={{0,2},{1,3},{2,0},{3,1},{4,6},{5,7},{6,4},{7,5},{8,10},{9,11},{10,... | collective-permute-start | bytes 3145736 | tf_op jit(solution)/shard_map/ppermute | solution.py:238
  (64 other events, 1019.2 us)
Sparse Core Ops, SparseCore 0:
  9.7 83.5 all-gather.3
  95.4 79.2 all-gather.5
  176.9 79.2 all-gather.7
  258.4 144.2 reduce-scatter.2
  404.9 77.4 reduce-scatter.4

commit v4 on v3

--- a/solution.py
+++ b/solution.py
@@ -548,7 +548,7 @@
         at += count
     grad_gain, grad_shift, grad_bqk, grad_bv, grad_bout, grad_bfc1 = vector_grads
 
-    first = gate(first, d_normed)
+    first = gate(first, mixed)
     if whole_heads:
         grad_wout = first[:, inner:].reshape(out_rows, width).astype(f32)
     grad_wqkv = to_rows(trade(first[:, :inner]), groups, 3 * heads)

time: 537 us -> 536 us (level)
  transfers between devices with their start and end apart: 43 -> 43, of which waited for: 20 -> 19; matrix products, arithmetic and copies ran while one was open for 31% -> 31% of each run, Pallas kernels for 21% -> 21%
where the time goes in v4:
time: 536 us; the launch traced here: 529 us
  waiting for transfers between devices  173 us (32%)
  Pallas kernels  115 us (21%)
  matrix products  89.5 us (17%)
  starting transfers between devices  51.8 us (10%)
  other arithmetic  46 us (9%)
  local copies, waits for them, and re-layouts  38.6 us (7%)
  between operations  15.2 us (3%)
    ppermute x32, waiting for transfers between devices, swap(): return lax.ppermute(value, axes, [(i, i ^ bit) for i in range(size)])  102 us
    dot_general x8, matrix products, dot(): lax.dot_general(a, b, (((ca,), (cb,)), ((), ())), preferred_element_type=...  89.5 us
    pallas_call x2, Pallas kernels, back_product(): pl.pallas_call(functools.partial(back_kernel, turned), grid_spec=pltpu.Pr...  43.5 us
    ppermute x32, starting transfers between devices, swap(): return lax.ppermute(value, axes, [(i, i ^ bit) for i in range(size)])  34.4 us
    pallas_call x1, Pallas kernels, attend_backward(): pl.pallas_call(functools.partial(backward_kernel, block), grid=(heads,),...  28 us
    all_gather x1, waiting for transfers between devices, local(): wfc2 = lax.all_gather(second_feed_weight, 'fsdp', axis=0, tiled=True)  21.8 us
    pallas_call x2, Pallas kernels, put_in_order(): pl.pallas_call(functools.partial(pieces_kernel, bool(vectors)), grid_spec...  21 us
    all_gather x1, waiting for transfers between devices, local(): first = lax.all_gather(gate(first, wfc1), 'fsdp', axis=0, tiled=True)  18.8 us
  transfers between devices with their start and end apart: 43, of which 19 were waited for; matrix products, arithmetic and copies ran while one was open for 31% of the time, Pallas kernels for 21%

profile of v4, /device:TPU:0, one launch (start us, length us, event | category | flops | bytes accessed | tf_op | source)
XLA Modules:
  0.0 529.1 jit_solution(2799117322874995420)
XLA Ops:
  12.5 21.9 %collective-permute-done.1.refs_2_ = bf16[256,2048]{1,0:T(8,128)(2,1)S(1)} collective-permute-done((bf16[256,2048]{1,0:T(8,128)(2,1)}, bf16[256,2048]{1,0:T(8,128)(2,1)S(1)}, u32[]{:S(2)}, u32[]{:S(2)}) %collective-permute-start.1) | collective-permute-done | bytes 1048608 | tf_op jit(solution)/shard_map/ppermute | solution.py:238
  55.6 11.9 %collective-permute-done.10 = bf16[2,4,704]{2,1,0:T(4,128)(2,1)S(1)} collective-permute-done((bf16[2,4,704]{2,1,0:T(4,128)(2,1)S(1)}, bf16[2,4,704]{2,1,0:T(4,128)(2,1)S(1)}, u32[]{:S(2)}, u32[]{:S(2)}) %collective-permute-start.10) | collective-permute-done | bytes 11296 | tf_op jit(solution)/shard_map/ppermute | solution.py:238
  71.5 21.8 %all-gather.4.cloned.1.call-done.refs_1_.wb_ref = bf16[1024,2048]{1,0:T(8,128)(2,1)} async-done(((bf16[256,2048]{1,0:T(8,128)(2,1)}), bf16[1024,2048]{1,0:T(8,128)(2,1)}) %all-gather.4.cloned.1.call-update) | async-done | bytes 4194320 | tf_op jit(solution)/shard_map/all_gather | solution.py:457
  94.2 12.9 %put_in_order.2 = (bf16[2048,2048]{1,0:T(8,128)(2,1)}, bf16[2048,2048]{1,0:T(8,128)(2,1)}) custom-call(s32[8]{0:T(128)S(1)} %stack.44.order_ref, bf16[256,2048]{1,0:T(8,128)(2,1)S(1)} %bitcast.128, bf16[256,2048]{1,0:T(8,128)(2,1)} %collective-permute-done.refs_1_, bf16[256,2048]{1,0:T(8,128)(2,1)S(1)} %collective-permute-done.1.refs_2_, ...), custom_call_target="tpu_custom_call" | custom-call | flops 11500000256 | bytes 1 | tf_op jit(solution)/shard_map/put_in_order/pallas_call | solution.py:316
  115.7 17.8 %collective-permute-done.13.refs_2_ = bf16[256,2048]{1,0:T(8,128)(2,1)S(1)} collective-permute-done((bf16[256,2048]{1,0:T(8,128)(2,1)}, bf16[256,2048]{1,0:T(8,128)(2,1)S(1)}, u32[]{:S(2)}, u32[]{:S(2)}) %collective-permute-start.13) | collective-permute-done | bytes 1048608 | tf_op jit(solution)/shard_map/ppermute | solution.py:238
  140.8 11.5 %collective-permute-done.17.refs_6_ = bf16[256,2048]{1,0:T(8,128)(2,1)} collective-permute-done((bf16[256,2048]{1,0:T(8,128)(2,1)S(1)}, bf16[256,2048]{1,0:T(8,128)(2,1)}, u32[]{:S(2)}, u32[]{:S(2)}) %collective-permute-start.17) | collective-permute-done | bytes 1048608 | tf_op jit(solution)/shard_map/ppermute | solution.py:284
  160.0 8.1 %put_in_order.3 = bf16[2048,2048]{1,0:T(8,128)(2,1)} custom-call(s32[8]{0:T(128)S(1)} %stack.44.order_ref, bf16[256,2048]{1,0:T(8,128)(2,1)S(1)} %copy-done.4, bf16[256,2048]{1,0:T(8,128)(2,1)} %collective-permute-done.12.refs_1_, bf16[256,2048]{1,0:T(8,128)(2,1)S(1)} %collective-permute-done.13.refs_2_, bf16[256,2048]{1,0:T(8,128)(2,1)} %collective-permute-done.14.refs_3_, ...), custom_call_target="tpu_custom_call" | custom-call | flops 11500000256 | bytes 1 | tf_op jit(solution)/shard_map/put_in_order/pallas_call | solution.py:316
  168.1 6.7 %all-gather.6.cloned.1.call-done.refs_1_.wb_ref = bf16[2048,1024]{1,0:T(8,128)(2,1)} async-done(((bf16[512,1024]{1,0:T(8,128)(2,1)}), bf16[2048,1024]{1,0:T(8,128)(2,1)}) %all-gather.6.cloned.1.call-update) | async-done | bytes 4194320 | tf_op jit(solution)/shard_map/all_gather | solution.py:459
  175.0 16.7 %multiply_convert_fusion = (bf16[1024,2048]{1,0:T(8,128)(2,1)}, f32[1024,2048]{1,0:T(8,128)S(1)}) fusion(f32[1024]{0:T(1024)S(1)} %bitcast.145, bf16[2048,1024]{1,0:T(8,128)(2,1)} %all-gather.6.cloned.1.call-done.refs_1_.wb_ref, bf16[2048,2048]{1,0:T(8,128)(2,1)} %get-tuple-element.25.refs_1_), kind=kOutput, calls=%fused_computation.13 | convolution fusion | flops 8610906112 | bytes 25169920 | tf_op jit(solution)/shard_map/dot_general | solution.py:20
  191.7 15.2 %convert_reduce_fusion = (f32[1024]{0:T(1024)S(1)}, bf16[1024,2048]{1,0:T(8,128)(2,1)}) fusion(f32[1024,2048]{1,0:T(8,128)S(1)} %get-tuple-element.72, f32[1024]{0:T(1024)S(1)} %bitcast.146, bf16[2048,2048]{1,0:T(8,128)(2,1)} %put_in_order.3, bf16[1024,2048]{1,0:T(8,128)(2,1)S(1)} %copy-done.27), kind=kOutput, calls=%fused_computation.10 | convolution fusion | flops 8636070912 | bytes 25174016 | tf_op jit(solution)/shard_map/dot_general | solution.py:20
  206.9 12.8 %convolution_convert_fusion.1 = bf16[2048,1024]{1,0:T(8,128)(2,1)S(1)} fusion(bf16[2048,2048]{1,0:T(8,128)(2,1)} %get-tuple-element.25.refs_1_, bf16[1024,2048]{1,0:T(8,128)(2,1)} %get-tuple-element.74.b_ref), kind=kOutput, calls=%fused_computation.16 | convolution fusion | flops 8592031744 | bytes 16777216 | tf_op jit(solution)/shard_map/dot_general | solution.py:20
  221.9 11.2 %convolution_convert_fusion = bf16[1024,2048]{1,0:T(8,128)(2,1)S(1)} fusion(bf16[1024,2048]{1,0:T(8,128)(2,1)S(1)} %copy-done.46, bf16[2048,2048]{1,0:T(8,128)(2,1)} %put_in_order.3), kind=kOutput, calls=%fused_computation.15 | convolution fusion | flops 8592031744 | bytes 16777216 | tf_op jit(solution)/shard_map/dot_general | solution.py:20
  237.4 18.8 %all-gather.8.cloned.1.call-done.wa_ref = bf16[2048,1024]{1,0:T(8,128)(2,1)} async-done(((bf16[512,1024]{1,0:T(8,128)(2,1)}), bf16[2048,1024]{1,0:T(8,128)(2,1)}) %all-gather.8.cloned.1.call-update) | async-done | bytes 4194320 | tf_op jit(solution)/shard_map/all_gather | solution.py:463
  258.5 6.2 %convolution_convert_fusion.4.g_ref = bf16[256,2048]{1,0:T(8,128)(2,1)S(1)} fusion(bf16[256,2048]{1,0:T(8,128)(2,1)S(1)} %reshape.272.wa_ref, bf16[2048,2048]{1,0:T(8,128)(2,1)} %put_in_order.3), kind=kOutput, calls=%fused_computation.25 | convolution fusion | flops 2148007936 | bytes 10485760 | tf_op jit(solution)/shard_map/dot_general | solution.py:20
  264.7 11.1 %convolution_add_fusion.q_ref.k_ref.v_ref = f32[768,2048]{1,0:T(8,128)} fusion(bf16[2048,2048]{1,0:T(8,128)(2,1)} %get-tuple-element.25.refs_1_, bf16[2048,1024]{1,0:T(8,128)(2,1)S(1)} %copy-done.29, f32[768]{0:T(1024)S(1)} %add.178), kind=kOutput, calls=%fused_computation.17 | convolution fusion | flops 6444023808 | bytes 17829888 | tf_op jit(solution)/shard_map/dot_general | solution.py:20
  275.7 17.2 %attend_forward.1 = (bf16[256,2048]{1,0:T(8,128)(2,1)S(1)}, f32[4,1,2048]{2,1,0:T(1,128)S(1)}, bf16[3,4,64,2048]{3,2,1,0:T(8,128)(2,1)S(1)}) custom-call(f32[768,2048]{1,0:T(8,128)} %convolution_add_fusion.q_ref.k_ref.v_ref, f32[768,2048]{1,0:T(8,128)} %convolution_add_fusion.q_ref.k_ref.v_ref, f32[768,2048]{1,0:T(8,128)} %convolution_add_fusion.q_ref.k_ref.v_ref, ...), custom_call_target="tpu_custom_call" | custom-call | flops 19549999104 | bytes 1 | tf_op jit(solution)/shard_map/attend_forward/pallas_call | solution.py:72
  294.5 28.0 %attend_backward.1 = (bf16[3,4,64,2048]{3,2,1,0:T(8,128)(2,1)S(1)}, f32[3,4,64,128]{3,2,1,0:T(8,128)S(1)}) custom-call(bf16[3,4,64,2048]{3,2,1,0:T(8,128)(2,1)} %copy-done.11, bf16[256,2048]{1,0:T(8,128)(2,1)S(1)} %get-tuple-element.26.a_ref.o_ref, bf16[256,2048]{1,0:T(8,128)(2,1)S(1)} %convolution_convert_fusion.4.g_ref, ...), custom_call_target="tpu_custom_call" | custom-call | flops 32199999488 | bytes 1 | tf_op jit(solution)/shard_map/attend_backward/pallas_call | solution.py:142
  324.3 26.7 %back_product.3 = (bf16[4,256,2048]{2,1,0:T(8,128)(2,1)}, bf16[4,256,2048]{2,1,0:T(8,128)(2,1)}, f32[8,2048]{1,0:T(8,128)}) custom-call(s32[1]{0:T(128)} %bitcast.core_ref, bf16[768,2048]{1,0:T(8,128)(2,1)} %bitcast.130, bf16[2048,1024]{1,0:T(8,128)(2,1)} %all-gather.8.cloned.1.call-done.wa_ref, bf16[1024,2048]{1,0:T(8,128)(2,1)} %get-tuple-element.74.b_ref, ...), custom_call_target="tpu_custom_call" | custom-call | flops 31050000384 | bytes 1 | tf_op jit(solution)/shard_map/back_product/pallas_call | solution.py:197
  359.6 10.6 %convolution_convert_fusion.2 = bf16[2048,768]{1,0:T(8,128)(2,1)} fusion(bf16[2048,2048]{1,0:T(8,128)(2,1)} %get-tuple-element.25.refs_1_, bf16[768,2048]{1,0:T(8,128)(2,1)S(1)} %bitcast.131), kind=kOutput, calls=%fused_computation.18 | convolution fusion | flops 6444023808 | bytes 14680064 | tf_op jit(solution)/shard_map/dot_general | solution.py:20
  370.9 16.8 %back_product.2 = (bf16[4,256,2048]{2,1,0:T(8,128)(2,1)}, bf16[4,256,2048]{2,1,0:T(8,128)(2,1)}) custom-call(s32[1]{0:T(128)} %bitcast.core_ref, bf16[256,2048]{1,0:T(8,128)(2,1)} %copy-done.9, bf16[256,2048]{1,0:T(8,128)(2,1)} %copy-done.28, bf16[1024,2048]{1,0:T(8,128)(2,1)} %get-tuple-element.71.b_ref, ...), custom_call_target="tpu_custom_call" | custom-call | flops 19549999104 | bytes 1 | tf_op jit(solution)/shard_map/back_product/pallas_call | solution.py:197
  421.6 15.6 %collective-permute-done.27 = bf16[2,256,1024]{2,1,0:T(8,128)(2,1)} collective-permute-done((bf16[2,256,1024]{2,1,0:T(8,128)(2,1)}, bf16[2,256,1024]{2,1,0:T(8,128)(2,1)}, u32[]{:S(2)}, u32[]{:S(2)}) %collective-permute-start.27) | collective-permute-done | bytes 1048608 | tf_op jit(solution)/shard_map/ppermute | solution.py:238
  466.8 15.7 %collective-permute-done.22 = bf16[2,256,1024]{2,1,0:T(8,128)(2,1)S(1)} collective-permute-done((bf16[2,256,1024]{2,1,0:T(8,128)(2,1)S(1)}, bf16[2,256,1024]{2,1,0:T(8,128)(2,1)S(1)}, u32[]{:S(2)}, u32[]{:S(2)}) %collective-permute-start.22) | collective-permute-done | bytes 1048608 | tf_op jit(solution)/shard_map/ppermute | solution.py:238
  483.2 6.1 %collective-permute-done.20 = bf16[2,256,1024]{2,1,0:T(8,128)(2,1)S(1)} collective-permute-done((bf16[2,256,1024]{2,1,0:T(8,128)(2,1)S(1)}, bf16[2,256,1024]{2,1,0:T(8,128)(2,1)S(1)}, u32[]{:S(2)}, u32[]{:S(2)}) %collective-permute-start.20) | collective-permute-done | bytes 1048608 | tf_op jit(solution)/shard_map/ppermute | solution.py:238
  514.0 6.2 %all-to-all-done.3.g_ref = bf16[8,64,768]{2,1,0:T(8,128)(2,1)S(1)} async-done(((bf16[8,64,768]{2,1,0:T(8,128)(2,1)}), bf16[8,64,768]{2,1,0:T(8,128)(2,1)S(1)}, u32[]{:S(2)}, u32[]{:S(2)}) %all-to-all-start.3) | async-done | bytes 786464 | tf_op jit(solution)/shard_map/all_to_all | solution.py:401
  (295 shorter events, 166.7 us)
Async XLA Ops:
  7.3 86.0 %all-gather.4.cloned.1.call-start = ((), (), s32[]{:S(2)}) async-start(), calls=%async_computation.6 | async-start | bytes 5242880 | tf_op jit(solution)/shard_map/all_gather | solution.py:457
  8.0 26.4 %collective-permute-start.1 = (bf16[256,2048]{1,0:T(8,128)(2,1)}, bf16[256,2048]{1,0:T(8,128)(2,1)S(1)}, u32[]{:S(2)}, u32[]{:S(2)}) collective-permute-start(bf16[256,2048]{1,0:T(8,128)(2,1)} %bitcast.125), channel_id=1, source_target_pairs={{0,2},{1,3},{2,0},{3,1},{4,6},{5,7},{6,4},{7,5},{8,10},{9,11},{10,... | collective-permute-start | bytes 3145736 | tf_op jit(solution)/shard_map/ppermute | solution.py:238
  11.0 24.9 %collective-permute-start.3 = (bf16[256,2048]{1,0:T(8,128)(2,1)}, bf16[256,2048]{1,0:T(8,128)(2,1)}, u32[]{:S(2)}, u32[]{:S(2)}) collective-permute-start(bf16[256,2048]{1,0:T(8,128)(2,1)} %bitcast.126), channel_id=1, source_target_pairs={{0,4},{1,5},{2,6},{3,7},{4,0},{5,1},{6,2},{7,3},{8,12},{9,13},{10,... | collective-permute-start | bytes 3145736 | tf_op jit(solution)/shard_map/ppermute | solution.py:238
  47.5 46.6 %collective-permute-start = (bf16[256,2048]{1,0:T(8,128)(2,1)S(1)}, bf16[256,2048]{1,0:T(8,128)(2,1)}, u32[]{:S(2)}, u32[]{:S(2)}) collective-permute-start(bf16[256,2048]{1,0:T(8,128)(2,1)S(1)} %bitcast.127), channel_id=1, source_target_pairs={{0,1},{1,0},{2,3},{3,2},{4,5},{5,4},{6,7},{7,6},{8,9},{9,8},{10,11... | collective-permute-start | bytes 3145736 | tf_op jit(solution)/shard_map/ppermute | solution.py:238
  49.1 22.4 %all-to-all-start.1 = ((bf16[8,64,1024]{2,1,0:T(8,128)(2,1)}), bf16[8,64,1024]{2,1,0:T(8,128)(2,1)S(1)}, u32[]{:S(2)}, u32[]{:S(2)}) async-start(bf16[8,64,1024]{2,1,0:T(8,128)(2,1)} %regroup.5), calls=%async_computation.1 | async-start | bytes 2097152 | tf_op jit(solution)/shard_map/all_to_all | solution.py:401
  52.7 122.0 %all-gather.6.cloned.1.call-start = ((), (), s32[]{:S(2)}) async-start(), calls=%async_computation.7 | async-start | bytes 5242880 | tf_op jit(solution)/shard_map/all_gather | solution.py:459
  52.8 41.4 %collective-permute-start.2 = (bf16[256,2048]{1,0:T(8,128)(2,1)S(1)}, bf16[256,2048]{1,0:T(8,128)(2,1)}, u32[]{:S(2)}, u32[]{:S(2)}) collective-permute-start(bf16[256,2048]{1,0:T(8,128)(2,1)S(1)} %collective-permute-done.1.refs_2_), channel_id=1, source_target_pairs={{0,1},{1,0},{2,3},{3,2},{4,5},{5,4},{6,7},{7,6},{8,9},{9,8},{10,11... | collective-permute-start | bytes 3145736 | tf_op jit(solution)/shard_map/ppermute | solution.py:238
  53.3 40.9 %collective-permute-start.4 = (bf16[256,2048]{1,0:T(8,128)(2,1)}, bf16[256,2048]{1,0:T(8,128)(2,1)}, u32[]{:S(2)}, u32[]{:S(2)}) collective-permute-start(bf16[256,2048]{1,0:T(8,128)(2,1)} %collective-permute-done.3.refs_4_), channel_id=1, source_target_pairs={{0,1},{1,0},{2,3},{3,2},{4,5},{5,4},{6,7},{7,6},{8,9},{9,8},{10,11... | collective-permute-start | bytes 3145736 | tf_op jit(solution)/shard_map/ppermute | solution.py:238
  53.4 40.8 %collective-permute-start.6 = (bf16[256,2048]{1,0:T(8,128)(2,1)}, bf16[256,2048]{1,0:T(8,128)(2,1)}, u32[]{:S(2)}, u32[]{:S(2)}) collective-permute-start(bf16[256,2048]{1,0:T(8,128)(2,1)} %collective-permute-done.5.refs_6_), channel_id=1, source_target_pairs={{0,1},{1,0},{2,3},{3,2},{4,5},{5,4},{6,7},{7,6},{8,9},{9,8},{10,11... | collective-permute-start | bytes 3145736 | tf_op jit(solution)/shard_map/ppermute | solution.py:238
  107.1 26.3 %collective-permute-start.13 = (bf16[256,2048]{1,0:T(8,128)(2,1)}, bf16[256,2048]{1,0:T(8,128)(2,1)S(1)}, u32[]{:S(2)}, u32[]{:S(2)}) collective-permute-start(bf16[256,2048]{1,0:T(8,128)(2,1)} %gate.8.refs_0_), channel_id=1, source_target_pairs={{0,2},{1,3},{2,0},{3,1},{4,6},{5,7},{6,4},{7,5},{8,10},{9,11},{10,... | collective-permute-start | bytes 3145736 | tf_op jit(solution)/shard_map/ppermute | solution.py:238
  108.7 27.2 %collective-permute-start.15 = (bf16[256,2048]{1,0:T(8,128)(2,1)}, bf16[256,2048]{1,0:T(8,128)(2,1)}, u32[]{:S(2)}, u32[]{:S(2)}) collective-permute-start(bf16[256,2048]{1,0:T(8,128)(2,1)} %gate.8.refs_0_), channel_id=1, source_target_pairs={{0,4},{1,5},{2,6},{3,7},{4,0},{5,1},{6,2},{7,3},{8,12},{9,13},{10,... | collective-permute-start | bytes 3145736 | tf_op jit(solution)/shard_map/ppermute | solution.py:238
  111.2 46.5 %all-to-all-start = ((bf16[8,64,768]{2,1,0:T(8,128)(2,1)}), bf16[8,64,768]{2,1,0:T(8,128)(2,1)}, u32[]{:S(2)}, u32[]{:S(2)}) async-start(bf16[8,64,768]{2,1,0:T(8,128)(2,1)} %regroup.4), calls=%async_computation | async-start | bytes 1572864 | tf_op jit(solution)/shard_map/all_to_all | solution.py:401
  115.6 140.6 %all-gather.8.cloned.1.call-start = ((), (), s32[]{:S(2)}) async-start(), calls=%async_computation.8 | async-start | bytes 5242880 | tf_op jit(solution)/shard_map/all_gather | solution.py:463
  140.3 19.7 %collective-permute-start.12 = (bf16[256,2048]{1,0:T(8,128)(2,1)S(1)}, bf16[256,2048]{1,0:T(8,128)(2,1)}, u32[]{:S(2)}, u32[]{:S(2)}) collective-permute-start(bf16[256,2048]{1,0:T(8,128)(2,1)S(1)} %copy-done.4), channel_id=1, source_target_pairs={{0,1},{1,0},{2,3},{3,2},{4,5},{5,4},{6,7},{7,6},{8,9},{9,8},{10,11... | collective-permute-start | bytes 3145736 | tf_op jit(solution)/shard_map/ppermute | solution.py:238
  174.8 227.9 %reduce-scatter.3.cloned.1.call-start = ((), (), s32[]{:S(2)}) async-start(), calls=%async_computation.9 | async-start | bytes 10485760 | tf_op jit(solution)/shard_map/reduce_scatter | solution.py:483
  236.7 265.2 %reduce-scatter.5.cloned.1.call-start = ((), (), s32[]{:S(2)}) async-start(), calls=%async_computation.10 | async-start | bytes 5242880 | tf_op jit(solution)/shard_map/reduce_scatter | solution.py:511
  370.2 32.6 %collective-permute-start.24 = (bf16[4,256,2048]{2,1,0:T(8,128)(2,1)}, bf16[4,256,2048]{2,1,0:T(8,128)(2,1)}, u32[]{:S(2)}, u32[]{:S(2)}) collective-permute-start(bf16[4,256,2048]{2,1,0:T(8,128)(2,1)} %get-tuple-element.34), channel_id=1, source_target_pairs={{0,1},{1,0},{2,3},{3,2},{4,5},{5,4},{6,7},{7,6},{8,9},{9,8},{10,11... | collective-permute-start | bytes 12582920 | tf_op jit(solution)/shard_map/ppermute | solution.py:238
  395.3 57.8 %collective-permute-start.19 = (bf16[4,256,2048]{2,1,0:T(8,128)(2,1)}, bf16[4,256,2048]{2,1,0:T(8,128)(2,1)}, u32[]{:S(2)}, u32[]{:S(2)}) collective-permute-start(bf16[4,256,2048]{2,1,0:T(8,128)(2,1)} %get-tuple-element.28), channel_id=1, source_target_pairs={{0,1},{1,0},{2,3},{3,2},{4,5},{5,4},{6,7},{7,6},{8,9},{9,8},{10,11... | collective-permute-start | bytes 12582920 | tf_op jit(solution)/shard_map/ppermute | solution.py:238
  411.0 26.3 %collective-permute-start.27 = (bf16[2,256,1024]{2,1,0:T(8,128)(2,1)}, bf16[2,256,1024]{2,1,0:T(8,128)(2,1)}, u32[]{:S(2)}, u32[]{:S(2)}) collective-permute-start(bf16[2,256,1024]{2,1,0:T(8,128)(2,1)} %fusion.24), channel_id=1, source_target_pairs={{0,4},{1,5},{2,6},{3,7},{4,0},{5,1},{6,2},{7,3},{8,12},{9,13},{10,... | collective-permute-start | bytes 3145736 | tf_op jit(solution)/shard_map/ppermute | solution.py:238
  414.4 28.1 %collective-permute-start.25 = (bf16[2,256,1024]{2,1,0:T(8,128)(2,1)}, bf16[2,256,1024]{2,1,0:T(8,128)(2,1)}, u32[]{:S(2)}, u32[]{:S(2)}) collective-permute-start(bf16[2,256,1024]{2,1,0:T(8,128)(2,1)} %fusion.26), channel_id=1, source_target_pairs={{0,2},{1,3},{2,0},{3,1},{4,6},{5,7},{6,4},{7,5},{8,10},{9,11},{10,... | collective-permute-start | bytes 3145736 | tf_op jit(solution)/shard_map/ppermute | solution.py:238
  417.0 35.2 %all-to-all-start.2 = ((bf16[8,64,1024]{2,1,0:T(8,128)(2,1)}), bf16[8,64,1024]{2,1,0:T(8,128)(2,1)S(1)}, u32[]{:S(2)}, u32[]{:S(2)}) async-start(bf16[8,64,1024]{2,1,0:T(8,128)(2,1)} %bitcast.142), calls=%async_computation.3 | async-start | bytes 2097152 | tf_op jit(solution)/shard_map/all_to_all | solution.py:401
  440.5 21.3 %collective-permute-start.28 = (bf16[256,1024]{1,0:T(8,128)(2,1)}, bf16[256,1024]{1,0:T(8,128)(2,1)}, u32[]{:S(2)}, u32[]{:S(2)}) collective-permute-start(bf16[256,1024]{1,0:T(8,128)(2,1)} %fusion.30), channel_id=1, source_target_pairs={{0,2},{1,3},{2,0},{3,1},{4,6},{5,7},{6,4},{7,5},{8,10},{9,11},{10,... | collective-permute-start | bytes 1572872 | tf_op jit(solution)/shard_map/ppermute | solution.py:238
  460.4 22.2 %collective-permute-start.22 = (bf16[2,256,1024]{2,1,0:T(8,128)(2,1)S(1)}, bf16[2,256,1024]{2,1,0:T(8,128)(2,1)S(1)}, u32[]{:S(2)}, u32[]{:S(2)}) collective-permute-start(bf16[2,256,1024]{2,1,0:T(8,128)(2,1)S(1)} %fusion.23), channel_id=1, source_target_pairs={{0,4},{1,5},{2,6},{3,7},{4,0},{5,1},{6,2},{7,3},{8,12},{9,13},{10,... | collective-permute-start | bytes 3145736 | tf_op jit(solution)/shard_map/ppermute | solution.py:238
  463.2 26.2 %collective-permute-start.20 = (bf16[2,256,1024]{2,1,0:T(8,128)(2,1)S(1)}, bf16[2,256,1024]{2,1,0:T(8,128)(2,1)S(1)}, u32[]{:S(2)}, u32[]{:S(2)}) collective-permute-start(bf16[2,256,1024]{2,1,0:T(8,128)(2,1)S(1)} %fusion.25), channel_id=1, source_target_pairs={{0,2},{1,3},{2,0},{3,1},{4,6},{5,7},{6,4},{7,5},{8,10},{9,11},{10,... | collective-permute-start | bytes 3145736 | tf_op jit(solution)/shard_map/ppermute | solution.py:238
  (66 other events, 1028.2 us)
Sparse Core Ops, SparseCore 0:
  9.7 83.5 all-gather.3
  95.4 79.2 all-gather.5
  176.9 79.2 all-gather.7
  258.4 144.2 reduce-scatter.2
  404.9 77.4 reduce-scatter.4
